TPU v7x, 32 devices: a whole 2x2x4 slice. The times are simulated.
32 devices in a mesh: batch: 4 (over z), ha: 4 (over y, x), wa: 2 (over core).
Axes of the slice: x: 2, y: 2, z: 4, core: 2. Of those that a mesh axis runs over, the one named last changes fastest.
Arguments:
- block_input: bfloat16 [32, 8, 12, 10, 256], P('batch', None, 'ha', 'wa'), may hold values from -6 to 6
- cotangent: bfloat16 [32, 8, 12, 10, 256], P('batch', None, 'ha', 'wa'), may hold values from -6 to 6
- frame_sides: int32 [4], P('batch'), may hold values from 7 to 10, as said below
- owner_list: int32 [1728, 1], replicated, may hold values from 0 to 31; in each aligned block of 1728 rows (0 to 1727, 1728 to 3455, ...) at most 55 rows name the same one
- master_slots: float32 [1760, 2048], P(('batch', 'ha', 'wa')), may hold values from -0.125 to 0.125
- first_slots: float32 [1760, 2048], P(('batch', 'ha', 'wa')), may hold values from -320 to 320
- second_slots: float32 [1760, 2048], P(('batch', 'ha', 'wa')), may hold values from 3072 to 12288
- norm_gains: float32 [1664], replicated, may hold values from 0.25 to 1.75
- norm_biases: float32 [1664], replicated, may hold values from -3 to 3
- norm_first: float32 [2, 1664], replicated, may hold values from -320 to 320
- norm_second: float32 [2, 1664], replicated, may hold values from 3072 to 12288
Outputs:
- block_output: float32 [32, 8, 12, 10, 256], P('batch', None, 'ha', 'wa')
- input_grad: float32 [32, 8, 12, 10, 256], P('batch', None, 'ha', 'wa')
- master_new: float32 [1760, 2048], P(('batch', 'ha', 'wa'))
- first_new: float32 [1760, 2048], P(('batch', 'ha', 'wa'))
- second_new: float32 [1760, 2048], P(('batch', 'ha', 'wa'))
- weight_copy: bfloat16 [1760, 2048], P(('batch', 'ha', 'wa'))
- norm_first_new: float32 [2, 1664], replicated
- norm_second_new: float32 [2, 1664], replicated
- norm_new: float32 [2, 1664], replicated
Inputs may be any that keep to these rules, and one draw needn't show every extreme that they name: `owner_list`: every device owns at least one piece and at most 55; some device owns exactly 55. `frame_sides`: each entry is 7 or 10, and both occur.
All inputs are finite; a program needn't handle non-finite values.
Results may differ from a plain program's by a relative error of at most 0.012.
The roundings to bfloat16 on the way count: a program that leaves them out, or rounds other values in their place, can miss the bound.
Values may be sent and summed in bfloat16 or wider, within the bound.
No kernel may reach another device: no remote copies, remote signals or barrier semaphores. Data moves between devices by JAX's collectives and lax.ppermute only.
A program may use at most 192 MiB of HBM per device.

v0:
```python
import math

import jax
import jax.numpy as jnp
from jax import lax
from jax.sharding import PartitionSpec as P

STEP = 5


EPSILON = 1e-05
ADAM_EPSILON = 1e-08
DECAY_RATE = 0.1
NORM_RATE = 0.3


def with_halo(block, sides, width):
    for axis, dim in sides:
        count = lax.axis_size(axis)
        forward = [(i, i + 1) for i in range(count - 1)]
        backward = [(target, source) for source, target in forward]
        low = lax.ppermute(
            lax.slice_in_dim(block, block.shape[dim] - width, None, axis=dim), axis, forward
        )
        high = lax.ppermute(lax.slice_in_dim(block, 0, width, axis=dim), axis, backward)
        block = jnp.concatenate([low, block, high], axis=dim)
    return block


def smooth_grad(values):
    sigma = jax.nn.sigmoid(values)
    return sigma * (1.0 + values * (1.0 - sigma))


def slot_of_pieces(owner_list, slot_count, device_total):
    owner_ids = owner_list[:, 0]
    onehot = (owner_ids[:, None] == jnp.arange(device_total, dtype=jnp.int32)[None, :]).astype(
        jnp.int32
    )
    earlier = jnp.cumsum(onehot, axis=0) - onehot
    ranking = jnp.sum(earlier * onehot, axis=1)
    return owner_ids * slot_count + ranking


def spatial_columns(padded, flipped):
    tile_rows = padded.shape[2] - 2
    tile_cols = padded.shape[3] - 2
    windows = []
    for row_tap in range(3):
        for col_tap in range(3):
            first_row = 2 - row_tap if flipped else row_tap
            first_col = 2 - col_tap if flipped else col_tap
            windows.append(
                padded[
                    :, :, first_row : first_row + tile_rows, first_col : first_col + tile_cols, :
                ]
            )
    joined = jnp.concatenate(windows, axis=-1)
    return joined.reshape(-1, joined.shape[-1])


def temporal_columns(values, flipped):
    frames = values.shape[1]
    padded = jnp.pad(values, ((0, 0), (1, 1), (0, 0), (0, 0), (0, 0)))
    windows = []
    for offset in range(3):
        first_frame = 2 - offset if flipped else offset
        windows.append(padded[:, first_frame : first_frame + frames])
    joined = jnp.concatenate(windows, axis=-1)
    return joined.reshape(-1, joined.shape[-1])


def norm_forward(values, valid_mask, cell_count, norm_gain, norm_bias):
    channel_mean = (
        lax.psum(jnp.sum(values * valid_mask, axis=(0, 1, 2, 3)), ("batch", "ha", "wa"))
        / cell_count
    )
    centered = (values - channel_mean) * valid_mask
    variance = (
        lax.psum(jnp.sum(centered * centered, axis=(0, 1, 2, 3)), ("batch", "ha", "wa"))
        / cell_count
    )
    inverse_std = lax.rsqrt(variance + EPSILON)
    normal = (values - channel_mean) * inverse_std
    return (normal * norm_gain + norm_bias, normal, inverse_std)


def norm_backward(upstream, normal, inverse_std, norm_gain, valid_mask, cell_count):
    bias_grad, gain_grad = lax.psum(
        (jnp.sum(upstream, axis=(0, 1, 2, 3)), jnp.sum(upstream * normal, axis=(0, 1, 2, 3))),
        ("batch", "ha", "wa"),
    )
    result = (
        inverse_std
        * norm_gain
        * (upstream - valid_mask * (bias_grad + normal * gain_grad) / cell_count)
    )
    return (result, gain_grad, bias_grad)


def per_device(
    block_input,
    cotangent,
    frame_sides,
    owner_list,
    master_slots,
    first_slots,
    second_slots,
    norm_gains,
    norm_biases,
    norm_first,
    norm_second,
):
    clip_count, frames, tile_rows, tile_cols, model_width = block_input.shape
    device_total = lax.axis_size(("batch", "ha", "wa"))
    slot_count, piece_len = master_slots.shape
    piece_total = owner_list.shape[0]
    middle = norm_gains.shape[0] // 2 - model_width
    all_sides = lax.all_gather(frame_sides, "batch", axis=0, tiled=True)
    cell_count = clip_count * frames * jnp.sum(all_sides * all_sides).astype(jnp.float32)
    own_side = frame_sides[0]
    row_ids = lax.axis_index("ha") * tile_rows + jnp.arange(tile_rows, dtype=jnp.int32)
    col_ids = lax.axis_index("wa") * tile_cols + jnp.arange(tile_cols, dtype=jnp.int32)
    grid_rows = tile_rows * lax.axis_size("ha")
    grid_cols = tile_cols * lax.axis_size("wa")
    valid_mask = (
        (row_ids[:, None] >= grid_rows - own_side) & (col_ids[None, :] >= grid_cols - own_side)
    ).astype(jnp.float32)[None, None, :, :, None]
    slot_index = slot_of_pieces(owner_list, slot_count, device_total)
    all_weights = lax.all_gather(
        master_slots.astype(jnp.bfloat16), ("batch", "ha", "wa"), axis=0, tiled=True
    )
    flat_weights = jnp.take(all_weights, slot_index, axis=0).reshape(-1)
    spatial_len = 9 * model_width * middle
    temporal_len = 3 * middle * model_width
    second_base = spatial_len + temporal_len
    spatial_one = flat_weights[:spatial_len].reshape(9 * model_width, middle)
    temporal_one = flat_weights[spatial_len:second_base].reshape(3 * middle, model_width)
    spatial_two = flat_weights[second_base : second_base + spatial_len].reshape(
        9 * model_width, middle
    )
    temporal_two = flat_weights[second_base + spatial_len : 2 * second_base].reshape(
        3 * middle, model_width
    )
    bounds = [
        0,
        middle,
        middle + model_width,
        2 * middle + model_width,
        2 * middle + 2 * model_width,
    ]
    mid_shape = (clip_count, frames, tile_rows, tile_cols, middle)
    wide_shape = (clip_count, frames, tile_rows, tile_cols, model_width)

    def unit_forward(low_input, spatial_w, temporal_w, index):
        padded = with_halo(low_input, (("ha", 2), ("wa", 3)), 1)
        columns_a = spatial_columns(padded, False)
        spatial = jnp.dot(columns_a, spatial_w, preferred_element_type=jnp.float32).reshape(
            mid_shape
        )
        normed_a, normal_a, inverse_a = norm_forward(
            spatial,
            valid_mask,
            cell_count,
            norm_gains[bounds[index] : bounds[index + 1]],
            norm_biases[bounds[index] : bounds[index + 1]],
        )
        inner_low = (jax.nn.silu(normed_a) * valid_mask).astype(jnp.bfloat16)
        columns_b = temporal_columns(inner_low, False)
        temporal = jnp.dot(columns_b, temporal_w, preferred_element_type=jnp.float32).reshape(
            wide_shape
        )
        normed_b, normal_b, inverse_b = norm_forward(
            temporal,
            valid_mask,
            cell_count,
            norm_gains[bounds[index + 1] : bounds[index + 2]],
            norm_biases[bounds[index + 1] : bounds[index + 2]],
        )
        return (
            normed_b,
            (columns_a, normed_a, normal_a, inverse_a, columns_b, normal_b, inverse_b),
        )

    def unit_backward(upstream, saved, spatial_w, temporal_w, index):
        columns_a, normed_a, normal_a, inverse_a, columns_b, normal_b, inverse_b = saved
        grad_t, gain_b, bias_b = norm_backward(
            upstream,
            normal_b,
            inverse_b,
            norm_gains[bounds[index + 1] : bounds[index + 2]],
            valid_mask,
            cell_count,
        )
        grad_t_low = grad_t.astype(jnp.bfloat16)
        temporal_grad = lax.dot_general(
            columns_b,
            grad_t_low.reshape(-1, model_width),
            (((0,), (0,)), ((), ())),
            preferred_element_type=jnp.float32,
        )
        back_b = temporal_columns(grad_t_low, True).reshape(-1, 3, model_width)
        grad_inner = jnp.einsum(
            "rkc,kic->ri",
            back_b,
            temporal_w.reshape(3, middle, model_width),
            preferred_element_type=jnp.float32,
        ).reshape(mid_shape)
        upstream_a = grad_inner * valid_mask * smooth_grad(normed_a)
        grad_s, gain_a, bias_a = norm_backward(
            upstream_a,
            normal_a,
            inverse_a,
            norm_gains[bounds[index] : bounds[index + 1]],
            valid_mask,
            cell_count,
        )
        grad_s_low = grad_s.astype(jnp.bfloat16)
        spatial_grad = lax.dot_general(
            columns_a,
            grad_s_low.reshape(-1, middle),
            (((0,), (0,)), ((), ())),
            preferred_element_type=jnp.float32,
        )
        padded_grad = with_halo(grad_s_low, (("ha", 2), ("wa", 3)), 1)
        back_a = spatial_columns(padded_grad, True).reshape(-1, 9, middle)
        grad_input = jnp.einsum(
            "rkc,kic->ri",
            back_a,
            spatial_w.reshape(9, model_width, middle),
            preferred_element_type=jnp.float32,
        ).reshape(wide_shape)
        return (grad_input, spatial_grad, temporal_grad, (gain_a, gain_b), (bias_a, bias_b))

    start = block_input.astype(jnp.float32) * valid_mask
    normed_one, saved_one = unit_forward(start.astype(jnp.bfloat16), spatial_one, temporal_one, 0)
    first_out = jax.nn.silu(normed_one) * valid_mask
    normed_two, saved_two = unit_forward(
        first_out.astype(jnp.bfloat16), spatial_two, temporal_two, 2
    )
    pre_act = normed_two + start
    block_output = jax.nn.silu(pre_act) * valid_mask
    top_grad = cotangent.astype(jnp.float32) * valid_mask * smooth_grad(pre_act)
    grad_first, spatial_grad_two, temporal_grad_two, gains_two, biases_two = unit_backward(
        top_grad, saved_two, spatial_two, temporal_two, 2
    )
    upstream_one = grad_first * valid_mask * smooth_grad(normed_one)
    grad_start, spatial_grad_one, temporal_grad_one, gains_one, biases_one = unit_backward(
        upstream_one, saved_one, spatial_one, temporal_one, 0
    )
    input_grad = (grad_start + top_grad) * valid_mask
    grad_flat = jnp.concatenate(
        [
            spatial_grad_one.reshape(-1, piece_len),
            temporal_grad_one.reshape(-1, piece_len),
            spatial_grad_two.reshape(-1, piece_len),
            temporal_grad_two.reshape(-1, piece_len),
        ],
        axis=0,
    )
    inverse_slots = (
        jnp.full((device_total * slot_count,), piece_total, jnp.int32)
        .at[slot_index]
        .set(jnp.arange(piece_total, dtype=jnp.int32))
    )
    grad_mine = lax.psum_scatter(
        jnp.take(grad_flat, inverse_slots, axis=0, mode="fill", fill_value=0.0),
        ("batch", "ha", "wa"),
        scatter_dimension=0,
        tiled=True,
    )
    correction = 1.0 - 0.5**STEP
    step_rate = 1.8 / math.sqrt(9.0 * model_width)
    first_new = 0.5 * first_slots + 0.5 * grad_mine
    second_new = 0.5 * second_slots + 0.5 * grad_mine * grad_mine
    master_new = master_slots - step_rate * (
        first_new / correction / (jnp.sqrt(second_new / correction) + ADAM_EPSILON)
        + DECAY_RATE * master_slots
    )
    weight_copy = master_new.astype(jnp.bfloat16)
    gain_grads = jnp.concatenate([gains_one[0], gains_one[1], gains_two[0], gains_two[1]])
    bias_grads = jnp.concatenate([biases_one[0], biases_one[1], biases_two[0], biases_two[1]])
    norm_grad = jnp.stack([gain_grads, bias_grads])
    norm_pair = jnp.stack([norm_gains, norm_biases])
    norm_first_new = 0.5 * norm_first + 0.5 * norm_grad
    norm_second_new = 0.5 * norm_second + 0.5 * norm_grad * norm_grad
    norm_new = norm_pair - NORM_RATE * (norm_first_new / correction) / (
        jnp.sqrt(norm_second_new / correction) + ADAM_EPSILON
    )
    return (
        block_output,
        input_grad,
        master_new,
        first_new,
        second_new,
        weight_copy,
        norm_first_new,
        norm_second_new,
        norm_new,
    )


def solution(mesh):
    return jax.shard_map(
        per_device,
        mesh=mesh,
        in_specs=(
            P("batch", None, "ha", "wa", None),
            P("batch", None, "ha", "wa", None),
            P("batch"),
            P(),
            P(("batch", "ha", "wa"), None),
            P(("batch", "ha", "wa"), None),
            P(("batch", "ha", "wa"), None),
            P(),
            P(),
            P(),
            P(),
        ),
        out_specs=(
            P("batch", None, "ha", "wa", None),
            P("batch", None, "ha", "wa", None),
            P(("batch", "ha", "wa"), None),
            P(("batch", "ha", "wa"), None),
            P(("batch", "ha", "wa"), None),
            P(("batch", "ha", "wa"), None),
            P(),
            P(),
            P(),
        ),
        check_vma=False,
    )
```

profile of v0, /device:TPU:0, one launch (start us, length us, event | category | flops | bytes accessed | tf_op | source)
XLA Modules:
  0.0 1205.4 jit_solution(13115558940644535587)
XLA Ops:
  18.5 8.5 all-reduce.5
  27.2 9.1 reduce-window.6
  44.1 8.9 scatter_custom_fusion
  61.2 26.7 %all-gather.3.cloned.1.call-done = bf16[32,55,2048]{2,1,0:T(8,128)(2,1)} async-done(((bf16[1,55,2048]{2,1,0:T(8,128)(2,1)}), bf16[32,55,2048]{2,1,0:T(8,128)(2,1)}) %all-gather.3.cloned.1.call-update) | async-done | bytes 7208976 | tf_op jit(solution)/shard_map/all_gather | solution.py:130
  95.2 18.5 %gather_fusion = bf16[1728,2048]{1,0:T(8,128)(2,1)} fusion(bf16[1760,2048]{1,0:T(8,128)(2,1)} %reshape.221, s32[2048]{0:T(1024)S(1)} %pad_clamp_fusion.1), kind=kCustom, calls=%fused_computation | custom fusion | bytes 14162688 | tf_op jit(solution)/shard_map/jit(_take)/gather | solution.py:133
  128.0 8.8 multiply_reduce_fusion.5
  136.8 39.7 %psum.112 = f32[576]{0:T(1024)S(1)} all-reduce(f32[576]{0:T(1024)} %get-tuple-element.105), channel_id=1, replica_groups=mesh['batch'=4,'ha'=4,'wa'=2] {'batch','ha','wa'}, use_global_device_ids=true, to_apply=%region_4.5 | all-reduce | flops 576 | bytes 4608 | tf_op jit(solution)/shard_map/psum | solution.py:75
  178.6 40.1 %psum.113 = f32[576]{0:T(1024)S(1)} all-reduce(f32[576]{0:T(1024)S(1)} %multiply_reduce_fusion.4), channel_id=1, replica_groups=mesh['batch'=4,'ha'=4,'wa'=2] {'batch','ha','wa'}, use_global_device_ids=true, to_apply=%region_7.8 | all-reduce | flops 576 | bytes 4608 | tf_op jit(solution)/shard_map/psum | solution.py:80
  231.4 40.1 %psum.114 = f32[256]{0:T(256)S(1)} all-reduce(f32[256]{0:T(256)S(1)} %get-tuple-element.107), channel_id=1, replica_groups=mesh['batch'=4,'ha'=4,'wa'=2] {'batch','ha','wa'}, use_global_device_ids=true, to_apply=%region_9.10 | all-reduce | flops 256 | bytes 2048 | tf_op jit(solution)/shard_map/psum | solution.py:75
  271.7 40.0 %psum.115 = f32[256]{0:T(256)S(1)} all-reduce(f32[256]{0:T(256)S(1)} %multiply_reduce_fusion.10), channel_id=1, replica_groups=mesh['batch'=4,'ha'=4,'wa'=2] {'batch','ha','wa'}, use_global_device_ids=true, to_apply=%region_11.12 | all-reduce | flops 256 | bytes 2048 | tf_op jit(solution)/shard_map/psum | solution.py:80
  365.6 39.5 %psum.116 = f32[576]{0:T(1024)S(1)} all-reduce(f32[576]{0:T(1024)S(1)} %get-tuple-element.109), channel_id=1, replica_groups=mesh['batch'=4,'ha'=4,'wa'=2] {'batch','ha','wa'}, use_global_device_ids=true, to_apply=%region_13.14 | all-reduce | flops 576 | bytes 4608 | tf_op jit(solution)/shard_map/psum | solution.py:75
  405.6 40.5 %psum.117 = f32[576]{0:T(1024)S(1)} all-reduce(f32[576]{0:T(1024)S(1)} %multiply_reduce_fusion.2), channel_id=1, replica_groups=mesh['batch'=4,'ha'=4,'wa'=2] {'batch','ha','wa'}, use_global_device_ids=true, to_apply=%region_15.16 | all-reduce | flops 576 | bytes 4608 | tf_op jit(solution)/shard_map/psum | solution.py:80
  460.2 39.6 %psum.118 = f32[256]{0:T(256)S(1)} all-reduce(f32[256]{0:T(256)S(1)} %get-tuple-element.111), channel_id=1, replica_groups=mesh['batch'=4,'ha'=4,'wa'=2] {'batch','ha','wa'}, use_global_device_ids=true, to_apply=%region_17.18 | all-reduce | flops 256 | bytes 2048 | tf_op jit(solution)/shard_map/psum | solution.py:75
  500.1 40.4 %psum.119 = f32[256]{0:T(256)S(1)} all-reduce(f32[256]{0:T(256)S(1)} %multiply_reduce_fusion.8), channel_id=1, replica_groups=mesh['batch'=4,'ha'=4,'wa'=2] {'batch','ha','wa'}, use_global_device_ids=true, to_apply=%region_19.20 | all-reduce | flops 256 | bytes 2048 | tf_op jit(solution)/shard_map/psum | solution.py:80
  544.4 39.6 %all-reduce.11 = (f32[256]{0:T(256)S(1)}, f32[256]{0:T(256)S(1)}) all-reduce(f32[256]{0:T(256)S(1)} %get-tuple-element.16, f32[256]{0:T(256)S(1)} %get-tuple-element.15), channel_id=1, replica_groups=mesh['batch'=4,'ha'=4,'wa'=2] {'batch','ha','wa'}, use_global_device_ids=true, to_apply=%region_23.24 | all-reduce | flops 512 | bytes 4096 | tf_op jit(solution)/shard_map/psum | solution.py:89
  598.7 40.6 %all-reduce.10 = (f32[576]{0:T(1024)S(1)}, f32[576]{0:T(1024)S(1)}) all-reduce(f32[576]{0:T(1024)S(1)} %get-tuple-element.12, f32[576]{0:T(1024)S(1)} %get-tuple-element.11), channel_id=1, replica_groups=mesh['batch'=4,'ha'=4,'wa'=2] {'batch','ha','wa'}, use_global_device_ids=true, to_apply=%region_27.28 | all-reduce | flops 1152 | bytes 9216 | tf_op jit(solution)/shard_map/psum | solution.py:89
  648.2 8.8 convolution_bitcast_fusion
  688.2 17.0 %concatenate.133 = bf16[8,8,3,5,5184]{4,1,3,2,0:T(8,128)(2,1)} concatenate(bf16[8,8,3,5,576]{4,1,3,2,0:T(8,128)(2,1)} %get-tuple-element.115, bf16[8,8,3,5,576]{4,1,3,2,0:T(8,128)(2,1)} %get-tuple-element.74, bf16[8,8,3,5,576]{4,1,3,2,0:T(8,128)(2,1)} %get-tuple-element.56, bf16[8,8,3,5,576]{4,1,3,2,0:T(8,128)(2,1)} %get-tuple-element.116, ...), dimensions={4} | concatenate | bytes 19906560 | tf_op jit(solution)/shard_map/concatenate | solution.py:58
  705.2 10.5 copy.47
  715.7 28.1 %reshape_reshape.26 = bf16[960,9,576]{2,1,0:T(8,128)(2,1)} reshape(bf16[8,8,3,5,5184]{4,3,2,1,0:T(8,128)(2,1)} %copy.47) | data formatting | bytes 19906560 | tf_op jit(solution)/shard_map/reshape;reshape | solution.py:226
  743.9 22.8 %fusion.13 = f32[8,8,3,5,256]{4,3,2,1,0:T(8,128)S(1)} fusion(bf16[9,256,576]{2,1,0:T(8,128)(2,1)} %reshape_reshape.27, bf16[8,8,3,5,576,9]{4,5,3,2,1,0:T(8,128)(2,1)} %bitcast.109), kind=kOutput, calls=%fused_computation.48 | convolution fusion | flops 2548039680 | bytes 13590528 | tf_op jit(solution)/shard_map/rkc,kic->ri/dot_general | solution.py:227
  767.5 41.1 %all-reduce.9 = (f32[256]{0:T(256)S(1)}, f32[256]{0:T(256)S(1)}) all-reduce(f32[256]{0:T(256)S(1)} %get-tuple-element.14, f32[256]{0:T(256)S(1)} %get-tuple-element.13), channel_id=1, replica_groups=mesh['batch'=4,'ha'=4,'wa'=2] {'batch','ha','wa'}, use_global_device_ids=true, to_apply=%region_31.32 | all-reduce | flops 512 | bytes 4096 | tf_op jit(solution)/shard_map/psum | solution.py:89
  826.6 38.8 %all-reduce.8 = (f32[576]{0:T(1024)S(1)}, f32[576]{0:T(1024)S(1)}) all-reduce(f32[576]{0:T(1024)S(1)} %get-tuple-element.10, f32[576]{0:T(1024)S(1)} %get-tuple-element.9), channel_id=1, replica_groups=mesh['batch'=4,'ha'=4,'wa'=2] {'batch','ha','wa'}, use_global_device_ids=true, to_apply=%region_35.36 | all-reduce | flops 1152 | bytes 9216 | tf_op jit(solution)/shard_map/psum | solution.py:89
  869.6 8.8 convolution_bitcast_fusion.1
  893.3 9.9 pad_maximum_fusion
  903.2 19.3 %gather_fusion.1 = f32[1760,2048]{1,0:T(8,128)} fusion(f32[1728,2048]{1,0:T(8,128)} %pad_maximum_fusion, s32[2048]{0:T(1024)S(1)} %copy-done.40), kind=kCustom, calls=%fused_computation.1 | custom fusion | bytes 28842880 | tf_op jit(solution)/shard_map/jit(_take)/gather | solution.py:267
  922.5 11.3 broadcast_select_fusion
  933.8 158.6 %fusion = f32[56,2048]{1,0:T(8,128)S(1)} fusion(f32[1760,2048]{1,0:T(8,128)} %broadcast_select_fusion), kind=kCustom, calls=%all-reduce-scatter | all-reduce-scatter fusion | flops 3670017 | bytes 14876672
  1119.4 17.0 %concatenate.140 = bf16[8,8,3,5,5184]{4,1,3,2,0:T(8,128)(2,1)} concatenate(bf16[8,8,3,5,576]{4,1,3,2,0:T(8,128)(2,1)} %get-tuple-element.53, bf16[8,8,3,5,576]{4,1,3,2,0:T(8,128)(2,1)} %get-tuple-element.70, bf16[8,8,3,5,576]{4,1,3,2,0:T(8,128)(2,1)} %get-tuple-element.50, bf16[8,8,3,5,576]{4,1,3,2,0:T(8,128)(2,1)} %get-tuple-element.52, ...), dimensions={4} | concatenate | bytes 19906560 | tf_op jit(solution)/shard_map/concatenate | solution.py:58
  1136.4 10.5 copy.54
  1146.9 28.3 %reshape_reshape.30 = bf16[960,9,576]{2,1,0:T(8,128)(2,1)} reshape(bf16[8,8,3,5,5184]{4,3,2,1,0:T(8,128)(2,1)} %copy.54) | data formatting | bytes 19906560 | tf_op jit(solution)/shard_map/reshape;reshape | solution.py:226
  1175.2 21.7 %fusion.18 = f32[8,8,3,5,256]{4,3,2,1,0:T(8,128)S(1)} fusion(bf16[9,256,576]{2,1,0:T(8,128)(2,1)S(1)} %copy-done.17, bf16[8,8,3,5,576,9]{4,5,3,2,1,0:T(8,128)(2,1)} %bitcast.110), kind=kOutput, calls=%fused_computation.49 | convolution fusion | flops 2548039680 | bytes 13590528 | tf_op jit(solution)/shard_map/rkc,kic->ri/dot_general | solution.py:227
  (307 shorter events, 255.7 us)
Async XLA Ops:
  7.2 80.8 %all-gather.3.cloned.1.call-start = ((), (), s32[]{:S(2)}) async-start(), calls=%async_computation | async-start | bytes 7569408 | tf_op jit(solution)/shard_map/all_gather | solution.py:130
  9.8 629.6 %copy-start.25 = (f32[3,5]{1,0:T(4,128)}, f32[3,5]{1,0:T(4,128)S(1)}, u32[]{:S(2)}) copy-start(f32[3,5]{1,0:T(4,128)S(1)} %and_convert_fusion) | copy-start | bytes 184
  11.0 27.4 %collective-permute-start = (bf16[8,8,1,5,256]{4,1,3,2,0:T(8,128)(2,1)S(1)}, bf16[8,8,1,5,256]{4,1,3,2,0:T(8,128)(2,1)S(1)}, u32[]{:S(2)}, u32[]{:S(2)}) collective-permute-start(bf16[8,8,1,5,256]{4,1,3,2,0:T(8,128)(2,1)S(1)} %get-tuple-element.95), channel_id=1, source_target_pairs={{0,2},{2,4},{4,6},{1,3},{3,5},{5,7},{8,10},{10,12},{12,14},{9,11},... | collective-permute-start | bytes 491528 | tf_op jit(solution)/shard_map/ppermute | solution.py:22
  17.2 21.2 %collective-permute-start.1 = (bf16[8,8,1,5,256]{4,1,3,2,0:T(8,128)(2,1)S(1)}, bf16[8,8,1,5,256]{4,1,3,2,0:T(8,128)(2,1)S(1)}, u32[]{:S(2)}, u32[]{:S(2)}) collective-permute-start(bf16[8,8,1,5,256]{4,1,3,2,0:T(8,128)(2,1)S(1)} %get-tuple-element.96), channel_id=1, source_target_pairs={{2,0},{4,2},{6,4},{3,1},{5,3},{7,5},{10,8},{12,10},{14,12},{11,9},... | collective-permute-start | bytes 491528 | tf_op jit(solution)/shard_map/ppermute | solution.py:25
  37.7 181.6 %copy-start.46 = (f32[576]{0:T(1024)}, f32[576]{0:T(1024)S(1)}, u32[]{:S(2)}) copy-start(f32[576]{0:T(1024)S(1)} %get-tuple-element.100) | copy-start | bytes 6916
  38.4 14.7 %collective-permute-start.3 = (bf16[8,8,5,1,256]{4,1,3,2,0:T(8,128)(2,1)S(1)}, bf16[8,8,5,1,256]{4,1,3,2,0:T(8,128)(2,1)S(1)}, u32[]{:S(2)}, u32[]{:S(2)}) collective-permute-start(bf16[8,8,5,1,256]{4,1,3,2,0:T(8,128)(2,1)S(1)} %get-tuple-element.87), channel_id=1, source_target_pairs={{1,0},{3,2},{5,4},{7,6},{9,8},{11,10},{13,12},{15,14},{17,16},{19,... | collective-permute-start | bytes 491528 | tf_op jit(solution)/shard_map/ppermute | solution.py:25
  39.7 13.4 %collective-permute-start.2 = (bf16[8,8,5,1,256]{4,1,3,2,0:T(8,128)(2,1)S(1)}, bf16[8,8,5,1,256]{4,1,3,2,0:T(8,128)(2,1)S(1)}, u32[]{:S(2)}, u32[]{:S(2)}) collective-permute-start(bf16[8,8,5,1,256]{4,1,3,2,0:T(8,128)(2,1)S(1)} %get-tuple-element.88), channel_id=1, source_target_pairs={{0,1},{2,3},{4,5},{6,7},{8,9},{10,11},{12,13},{14,15},{16,17},{18,... | collective-permute-start | bytes 491528 | tf_op jit(solution)/shard_map/ppermute | solution.py:22
  136.8 82.5 %copy-start.3 = (f32[8,8,3,5,576]{4,1,3,2,0:T(8,128)S(1)}, f32[8,8,3,5,576]{4,1,3,2,0:T(8,128)}, u32[]{:S(2)}) copy-start(f32[8,8,3,5,576]{4,1,3,2,0:T(8,128)} %get-tuple-element.106) | copy-start | bytes 6635524
  228.1 84.2 %copy-start.51 = (f32[256]{0:T(256)S(1)}, f32[256]{0:T(256)}, u32[]{:S(2)}) copy-start(f32[256]{0:T(256)} %get-tuple-element.102) | copy-start | bytes 3076
  231.3 128.7 %copy-start = (f32[8,8,3,5,256]{4,1,3,2,0:T(8,128)}, f32[8,8,3,5,256]{4,1,3,2,0:T(8,128)S(1)}, u32[]{:S(2)}) copy-start(f32[8,8,3,5,256]{4,1,3,2,0:T(8,128)S(1)} %get-tuple-element.108) | copy-start | bytes 2949124
  231.3 100.4 %copy-start.34 = (f32[1664]{0:T(1024)S(1)}, f32[1664]{0:T(1024)}, u32[]{:S(2)}) copy-start(f32[1664]{0:T(1024)} %param.19) | copy-start | bytes 19972
  231.4 102.2 %copy-start.11 = (bf16[216,2048]{1,0:T(8,128)(2,1)S(1)}, bf16[216,2048]{1,0:T(8,128)(2,1)}, u32[]{:S(2)}) copy-start(bf16[216,2048]{1,0:T(8,128)(2,1)} %get-tuple-element.44) | copy-start | bytes 2654212
  271.5 88.6 %copy-start.38 = (f32[256]{0:T(256)}, f32[256]{0:T(256)S(1)}, u32[]{:S(2)}) copy-start(f32[256]{0:T(256)S(1)} %broadcast_divide_fusion.3) | copy-start | bytes 3076
  312.7 7.0 collective-permute-start.4
  316.9 7.6 collective-permute-start.5
  325.2 33.5 %collective-permute-start.7 = (bf16[8,8,5,1,256]{4,1,3,2,0:T(8,128)(2,1)}, bf16[8,8,5,1,256]{4,1,3,2,0:T(8,128)(2,1)}, u32[]{:S(2)}, u32[]{:S(2)}) collective-permute-start(bf16[8,8,5,1,256]{4,1,3,2,0:T(8,128)(2,1)} %get-tuple-element.83), channel_id=1, source_target_pairs={{1,0},{3,2},{5,4},{7,6},{9,8},{11,10},{13,12},{15,14},{17,16},{19,... | collective-permute-start | bytes 491528 | tf_op jit(solution)/shard_map/ppermute | solution.py:25
  326.5 32.2 %collective-permute-start.6 = (bf16[8,8,5,1,256]{4,1,3,2,0:T(8,128)(2,1)}, bf16[8,8,5,1,256]{4,1,3,2,0:T(8,128)(2,1)}, u32[]{:S(2)}, u32[]{:S(2)}) collective-permute-start(bf16[8,8,5,1,256]{4,1,3,2,0:T(8,128)(2,1)} %get-tuple-element.84), channel_id=1, source_target_pairs={{0,1},{2,3},{4,5},{6,7},{8,9},{10,11},{12,13},{14,15},{16,17},{18,... | collective-permute-start | bytes 491528 | tf_op jit(solution)/shard_map/ppermute | solution.py:22
  365.5 228.1 %copy-start.5 = (f32[8,8,3,5,576]{4,1,3,2,0:T(8,128)}, f32[8,8,3,5,576]{4,1,3,2,0:T(8,128)S(1)}, u32[]{:S(2)}) copy-start(f32[8,8,3,5,576]{4,1,3,2,0:T(8,128)S(1)} %get-tuple-element.110) | copy-start | bytes 6635524
  456.9 84.3 %copy-start.68 = (f32[256]{0:T(256)S(1)}, f32[256]{0:T(256)}, u32[]{:S(2)}) copy-start(f32[256]{0:T(256)} %get-tuple-element.103) | copy-start | bytes 3076
  642.6 14.3 %collective-permute-start.8 = (bf16[8,8,1,5,576]{4,1,3,2,0:T(8,128)(2,1)S(1)}, bf16[8,8,1,5,576]{4,1,3,2,0:T(8,128)(2,1)S(1)}, u32[]{:S(2)}, u32[]{:S(2)}) collective-permute-start(bf16[8,8,1,5,576]{4,1,3,2,0:T(8,128)(2,1)S(1)} %get-tuple-element.75), channel_id=1, source_target_pairs={{0,2},{2,4},{4,6},{1,3},{3,5},{5,7},{8,10},{10,12},{12,14},{9,11},... | collective-permute-start | bytes 1105928 | tf_op jit(solution)/shard_map/ppermute | solution.py:22
  646.9 17.5 %collective-permute-start.9 = (bf16[8,8,1,5,576]{4,1,3,2,0:T(8,128)(2,1)S(1)}, bf16[8,8,1,5,576]{4,1,3,2,0:T(8,128)(2,1)S(1)}, u32[]{:S(2)}, u32[]{:S(2)}) collective-permute-start(bf16[8,8,1,5,576]{4,1,3,2,0:T(8,128)(2,1)S(1)} %get-tuple-element.76), channel_id=1, source_target_pairs={{2,0},{4,2},{6,4},{3,1},{5,3},{7,5},{10,8},{12,10},{14,12},{11,9},... | collective-permute-start | bytes 1105928 | tf_op jit(solution)/shard_map/ppermute | solution.py:25
  665.4 17.6 %collective-permute-start.11 = (bf16[8,8,5,1,576]{4,1,3,2,0:T(8,128)(2,1)}, bf16[8,8,5,1,576]{4,1,3,2,0:T(8,128)(2,1)}, u32[]{:S(2)}, u32[]{:S(2)}) collective-permute-start(bf16[8,8,5,1,576]{4,1,3,2,0:T(8,128)(2,1)} %get-tuple-element.66), channel_id=1, source_target_pairs={{0,1},{2,3},{4,5},{6,7},{8,9},{10,11},{12,13},{14,15},{16,17},{18,... | collective-permute-start | bytes 1105928 | tf_op jit(solution)/shard_map/ppermute | solution.py:22
  667.5 15.6 %collective-permute-start.10 = (bf16[8,8,5,1,576]{4,1,3,2,0:T(8,128)(2,1)}, bf16[8,8,5,1,576]{4,1,3,2,0:T(8,128)(2,1)}, u32[]{:S(2)}, u32[]{:S(2)}) collective-permute-start(bf16[8,8,5,1,576]{4,1,3,2,0:T(8,128)(2,1)} %get-tuple-element.67), channel_id=1, source_target_pairs={{1,0},{3,2},{5,4},{7,6},{9,8},{11,10},{13,12},{15,14},{17,16},{19,... | collective-permute-start | bytes 1105928 | tf_op jit(solution)/shard_map/ppermute | solution.py:25
  879.9 220.6 %collective-permute-start.12 = (bf16[8,8,1,5,576]{4,1,3,2,0:T(8,128)(2,1)}, bf16[8,8,1,5,576]{4,1,3,2,0:T(8,128)(2,1)S(1)}, u32[]{:S(2)}, u32[]{:S(2)}) collective-permute-start(bf16[8,8,1,5,576]{4,1,3,2,0:T(8,128)(2,1)} %get-tuple-element.71), channel_id=1, source_target_pairs={{0,2},{2,4},{4,6},{1,3},{3,5},{5,7},{8,10},{10,12},{12,14},{9,11},... | collective-permute-start | bytes 1105928 | tf_op jit(solution)/shard_map/ppermute | solution.py:22
  884.1 216.4 %collective-permute-start.13 = (bf16[8,8,1,5,576]{4,1,3,2,0:T(8,128)(2,1)}, bf16[8,8,1,5,576]{4,1,3,2,0:T(8,128)(2,1)}, u32[]{:S(2)}, u32[]{:S(2)}) collective-permute-start(bf16[8,8,1,5,576]{4,1,3,2,0:T(8,128)(2,1)} %get-tuple-element.72), channel_id=1, source_target_pairs={{2,0},{4,2},{6,4},{3,1},{5,3},{7,5},{10,8},{12,10},{14,12},{11,9},... | collective-permute-start | bytes 1105928 | tf_op jit(solution)/shard_map/ppermute | solution.py:25
  933.8 164.8 %copy-start.42 = (f32[1,1664]{1,0:T(1,128)S(1)}, f32[1,1664]{1,0:T(1,128)}, u32[]{:S(2)}) copy-start(f32[1,1664]{1,0:T(1,128)} %stack.22) | copy-start | bytes 19972
  933.8 164.8 %copy-start.43 = (f32[1,1664]{1,0:T(1,128)S(1)}, f32[1,1664]{1,0:T(1,128)}, u32[]{:S(2)}) copy-start(f32[1,1664]{1,0:T(1,128)} %stack.21) | copy-start | bytes 19972
  933.8 164.8 %copy-start.60 = (f32[2,1664]{1,0:T(2,128)S(1)}, f32[2,1664]{1,0:T(2,128)}, u32[]{:S(2)}) copy-start(f32[2,1664]{1,0:T(2,128)} %param.21) | copy-start | bytes 39940
  933.8 164.8 %copy-start.61 = (f32[2,1664]{1,0:T(2,128)S(1)}, f32[2,1664]{1,0:T(2,128)}, u32[]{:S(2)}) copy-start(f32[2,1664]{1,0:T(2,128)} %param.20) | copy-start | bytes 39940
  1092.4 6.8 collective-permute-start.16
  1101.7 11.7 collective-permute-start.15
  1107.9 5.5 collective-permute-start.14
  (56 other events, 1150.2 us)
Sparse Core Ops, SparseCore 0:
  11.4 76.4 all-gather.2
where the time goes:
time: 1220 us; the launch traced here: 1210 us
  blocking collectives  647 us (53%)
  local copies, waits for them, and re-layouts  274 us (22%)
  matrix products  98.9 us (8%)
  other arithmetic  78 us (6%)
  starting transfers between devices  50 us (4%)
  waiting for transfers between devices  40.4 us (3%)
  between operations  16.7 us (1%)
    unnamed x2, blocking collectives  167 us
    psum x4, blocking collectives, norm_forward(): lax.psum(jnp.sum(centered * centered, axis=(0, 1, 2, 3)), ('batch', 'ha',...  161 us
    psum x4, blocking collectives, norm_backward(): lax.psum((jnp.sum(upstream, axis=(0, 1, 2, 3)), jnp.sum(upstream * normal...  160 us
    psum x4, blocking collectives, norm_forward(): lax.psum(jnp.sum(values * valid_mask, axis=(0, 1, 2, 3)), ('batch', 'ha',...  159 us
    another operation x2, local copies, waits for them, and re-layouts, unit_backward(): back_a = spatial_columns(padded_grad, True).reshape(-1, 9, middle)  56.4 us
    concatenate x6, local copies, waits for them, and re-layouts, spatial_columns(): joined = jnp.concatenate(windows, axis=-1)  55.9 us
    dot_general x2, matrix products, unit_backward(): jnp.einsum('rkc,kic->ri', back_a, spatial_w.reshape(9, model_width, middl...  44.5 us
    ppermute x8, starting transfers between devices, with_halo(): lax.ppermute(lax.slice_in_dim(block, block.shape[dim] - width, None, axis...  33.5 us
  transfers between devices with their start and end apart: 18, of which 4 were waited for; matrix products, arithmetic and copies ran while one was open for 24% of the time, Pallas kernels for 0%

commit v1 on v0

v1 whole, which is shorter than its diff:
```python
import functools
import math

import jax
import jax.numpy as jnp
from jax import lax
from jax.experimental import pallas as pl
from jax.experimental.pallas import tpu as pltpu
from jax.sharding import PartitionSpec as P

STEP = 5
EPSILON = 1e-05
ADAM_EPSILON = 1e-08
DECAY_RATE = 0.1
NORM_RATE = 0.3

AXES = ("batch", "ha", "wa")
F32 = jnp.float32
BF16 = jnp.bfloat16
VMEM = pl.BlockSpec(memory_space=pltpu.VMEM)
SMEM = pl.BlockSpec(memory_space=pltpu.SMEM)
CELL = 64
LANES = 128
PIECE_ROWS = 16


def sigmoid(v):
    return 1.0 / (1.0 + jnp.exp(-v))


def cell_rows(index, count=1):
    return pl.ds(pl.multiple_of(index * CELL, CELL), count * CELL)


def block_rows(index, size):
    return pl.ds(pl.multiple_of(index * size, size), size)


def fold8(block):
    return jnp.sum(block.reshape(-1, 8, block.shape[-1]), axis=0)


def widen(lane_block, width):
    return jnp.concatenate([lane_block] * (width // LANES), axis=1)


def valid_rows(valid_ref, cells):
    total = valid_ref[0]
    for cell in range(1, cells):
        total = total + valid_ref[cell]
    return total * CELL


def send_stats(values_ref, valid_ref, msg_ref):
    rows, width = values_ref.shape
    cells = rows // CELL
    count = valid_rows(valid_ref, cells)

    def add(cell, total):
        return total + valid_ref[cell] * fold8(values_ref[cell_rows(cell), :])

    total = lax.fori_loop(0, cells, add, jnp.zeros((8, width), F32))
    total = jnp.sum(total, axis=0, keepdims=True)
    mean = total / jnp.maximum(jnp.full((1, width), count, F32), 1.0)

    def add_squares(cell, squares):
        centered = values_ref[cell_rows(cell), :] - mean
        return squares + valid_ref[cell] * fold8(centered * centered)

    squares = lax.fori_loop(0, cells, add_squares, jnp.zeros((8, width), F32))
    squares = jnp.sum(squares, axis=0, keepdims=True)
    message = jnp.concatenate([total, squares, jnp.full((1, LANES), count, F32)], axis=1)
    msg_ref[...] = jnp.broadcast_to(message[None], msg_ref.shape)


def receive_stats(msg_ref):
    devices, _, length = msg_ref.shape
    width = (length - LANES) // 2

    def add(i, carry):
        total, count = carry
        return (total + msg_ref[i, :, :width], count + msg_ref[i, :, 2 * width :])

    total, count = lax.fori_loop(
        0, devices, add, (jnp.zeros((1, width), F32), jnp.zeros((1, LANES), F32)), unroll=4
    )
    count = widen(count, width)
    mean = total / count

    def add_squares(i, squares):
        own = widen(msg_ref[i, :, 2 * width :], width)
        offset = msg_ref[i, :, :width] / jnp.maximum(own, 1.0) - mean
        return squares + msg_ref[i, :, width : 2 * width] + own * offset * offset

    squares = lax.fori_loop(0, devices, add_squares, jnp.zeros((1, width), F32), unroll=4)
    return mean, lax.rsqrt(squares / count + EPSILON), count


def keep_stats(stats_ref, mean, rstd, count):
    stats_ref[0:1, :] = mean
    stats_ref[1:2, :] = rstd
    stats_ref[2:3, :] = count


def receive_sums(msg_ref):
    devices, _, length = msg_ref.shape
    total = lax.fori_loop(
        0, devices, lambda i, t: t + msg_ref[i], jnp.zeros((1, length), F32), unroll=4
    )
    return total[:, : length // 2], total[:, length // 2 :]


def send_sums(bias, gain, msg_ref):
    message = jnp.concatenate(
        [jnp.sum(bias, axis=0, keepdims=True), jnp.sum(gain, axis=0, keepdims=True)], axis=1
    )
    msg_ref[...] = jnp.broadcast_to(message[None], msg_ref.shape)


def later_frame(block):
    return jnp.concatenate([block[8:], jnp.zeros((8, block.shape[1]), block.dtype)], axis=0)


def earlier_frame(block):
    return jnp.concatenate([jnp.zeros((8, block.shape[1]), block.dtype), block[:-8]], axis=0)


def unpack_weights_kernel(slot_ref, all_ref, ws_ref, wt_ref, stage, turn, *, base):
    low = lax.broadcasted_iota(jnp.int32, (8, LANES), 1) < 64
    zero = jnp.zeros((8, LANES), F32)
    spatial_groups = ws_ref.shape[0] // 32

    def load_piece(number):
        start = pl.multiple_of(slot_ref[number] * PIECE_ROWS, PIECE_ROWS)
        return all_ref[pl.ds(start, PIECE_ROWS), :].astype(F32)

    def spatial_group(g, _):
        for q in range(9):
            stage[16 * q : 16 * q + 16, :] = load_piece(base + 9 * g + q)
        for i in range(2):
            a = [stage[pl.ds(72 * i + j, 8, stride=9), :] for j in range(9)]
            r = [pltpu.roll(a[4 + j], 64, axis=1) for j in range(5)]
            even = a[:4] + [jnp.where(low, a[4], zero)]
            odd = [jnp.where(low, r[j], r[j + 1]) for j in range(4)] + [jnp.where(low, r[4], zero)]
            for j in range(5):
                turn[j, pl.ds(16 * i, 8, stride=2), :] = even[j]
                turn[j, pl.ds(16 * i + 1, 8, stride=2), :] = odd[j]
        rows = block_rows(g, 32)
        for j in range(5):
            ws_ref[rows, LANES * j : LANES * (j + 1)] = turn[j].astype(BF16)
        return 0

    lax.fori_loop(0, spatial_groups, spatial_group, 0)
    temporal_base = base + 9 * spatial_groups
    padded = wt_ref.shape[0] // 3
    pairs = (9 * spatial_groups) // 3 // 6
    for tap in range(3):

        def temporal_pair(k, _):
            first = temporal_base + tap * 2 * pairs + 2 * k
            stage[0:16, :] = load_piece(first)
            stage[16:32, :] = load_piece(first + 1)
            rows = pl.ds(pl.multiple_of(tap * padded + k * 16, 16), 16)
            for h in range(2):
                wt_ref[rows, LANES * h : LANES * (h + 1)] = stage[pl.ds(h, 16, stride=2), :].astype(
                    BF16
                )
            return 0

        lax.fori_loop(0, pairs, temporal_pair, 0)
        wt_ref[tap * padded + 16 * pairs : (tap + 1) * padded, :] = jnp.zeros(
            (padded - 16 * pairs, wt_ref.shape[1]), BF16
        )


def pack_grads_kernel(slot_ref, ws_ref, wt_ref, ws2_ref, wt2_ref, out_ref, stage, turn):
    low = lax.broadcasted_iota(jnp.int32, (8, LANES), 1) < 64
    spatial_groups = ws_ref.shape[0] // 32
    padded = wt_ref.shape[0] // 3
    pairs = (9 * spatial_groups) // 3 // 6

    def clear(i, _):
        out_ref[block_rows(i, 32), :] = jnp.zeros((32, LANES), BF16)
        return 0

    lax.fori_loop(0, out_ref.shape[0] // 32, clear, 0)

    def store_piece(number, rows16):
        start = pl.multiple_of(slot_ref[number] * PIECE_ROWS, PIECE_ROWS)
        out_ref[pl.ds(start, PIECE_ROWS), :] = rows16.astype(BF16)

    base = 0
    for spatial, temporal in ((ws_ref, wt_ref), (ws2_ref, wt2_ref)):

        def spatial_group(g, _):
            rows = block_rows(g, 32)
            for j in range(5):
                turn[j] = spatial[rows, LANES * j : LANES * (j + 1)]
            for i in range(2):
                even = [turn[j, pl.ds(16 * i, 8, stride=2), :] for j in range(5)]
                odd = [turn[j, pl.ds(16 * i + 1, 8, stride=2), :] for j in range(5)]
                r = [pltpu.roll(odd[j], 64, axis=1) for j in range(5)]
                flat = even[:4] + [jnp.where(low, even[4], r[0])]
                flat += [jnp.where(low, r[j], r[j + 1]) for j in range(4)]
                for j in range(9):
                    stage[pl.ds(72 * i + j, 8, stride=9), :] = flat[j]
            for q in range(9):
                store_piece(base + 9 * g + q, stage[16 * q : 16 * q + 16, :])
            return 0

        lax.fori_loop(0, spatial_groups, spatial_group, 0)
        base += 9 * spatial_groups
        for tap in range(3):

            def temporal_pair(k, _):
                first = base + tap * 2 * pairs + 2 * k
                rows = pl.ds(pl.multiple_of(tap * padded + k * 16, 16), 16)
                for h in range(2):
                    stage[pl.ds(h, 16, stride=2), :] = temporal[rows, LANES * h : LANES * (h + 1)]
                store_piece(first, stage[0:16, :])
                store_piece(first + 1, stage[16:32, :])
                return 0

            lax.fori_loop(0, pairs, temporal_pair, 0)
        base += 6 * pairs


def fill_padded(place_ref, padded_ref, tile_ref, halo_refs):
    up, down, side, corner_up, corner_down = halo_refs
    rows, cols = tile_ref.shape[:2]
    padded_ref[1 : rows + 1, 1 : cols + 1] = tile_ref[...]
    padded_ref[0, 1 : cols + 1] = up[...]
    padded_ref[rows + 1, 1 : cols + 1] = down[...]
    for core in range(2):
        near, far = (cols + 1, 0) if core == 0 else (0, cols + 1)

        @pl.when(place_ref[0] == core)
        def _():
            padded_ref[1 : rows + 1, near] = side[...]
            padded_ref[0, near] = corner_up[...]
            padded_ref[rows + 1, near] = corner_down[...]
            padded_ref[:, far] = jnp.zeros((rows + 2,) + tile_ref.shape[2:], BF16)


def write_edges(place_ref, tile_ref, edge_refs):
    top, bottom, side, corner_top, corner_bottom = edge_refs
    rows, cols = tile_ref.shape[:2]
    top[...] = tile_ref[0]
    bottom[...] = tile_ref[rows - 1]
    edge = jnp.where(place_ref[0] == 0, cols - 1, 0)
    side[...] = tile_ref[:, edge]
    corner_top[...] = tile_ref[0, edge]
    corner_bottom[...] = tile_ref[rows - 1, edge]


def spatial_kernel(
    place_ref, valid_ref, tile_ref, up, down, side, cup, cdown, ws_ref, padded_ref, s_ref, msg_ref
):
    rows, cols, cell, width = tile_ref.shape
    fill_padded(place_ref, padded_ref, tile_ref, (up, down, side, cup, cdown))

    def one_row(r, _):
        windows = []
        for row_tap in range(3):
            for col_tap in range(3):
                window = padded_ref[r + row_tap, col_tap : col_tap + cols]
                windows.append(window.reshape(cols * cell, width))
        s_ref[block_rows(r, cols * cell), :] = jnp.dot(
            jnp.concatenate(windows, axis=1), ws_ref[...], preferred_element_type=F32
        )
        return 0

    lax.fori_loop(0, rows, one_row, 0)
    send_stats(s_ref, valid_ref, msg_ref)


def spatial_back(padded_ref, ws_ref, r, cols, cell, width):
    total = None
    for row_tap in range(3):
        for col_tap in range(3):
            window = padded_ref[r + 2 - row_tap, 2 - col_tap : 2 - col_tap + cols]
            tap = 3 * row_tap + col_tap
            term = lax.dot_general(
                window.reshape(cols * cell, window.shape[-1]),
                ws_ref[tap * width : (tap + 1) * width, :],
                (((1,), (1,)), ((), ())),
                preferred_element_type=F32,
            )
            total = term if total is None else total + term
    return total


def spatial_weight_kernel(padded_ref, ds_ref, grad_ref):
    rows, cols, cell, middle = ds_ref.shape
    width = padded_ref.shape[-1]
    grads = ds_ref[...].reshape(rows * cols * cell, middle)
    for row_tap in range(3):
        for col_tap in range(3):
            window = padded_ref[row_tap : row_tap + rows, col_tap : col_tap + cols]
            tap = 3 * row_tap + col_tap
            grad_ref[tap * width : (tap + 1) * width, :] = lax.dot_general(
                window.reshape(rows * cols * cell, width),
                grads,
                (((0,), (0,)), ((), ())),
                preferred_element_type=F32,
            )


def spatial_grad_kernel(
    place_ref, valid_ref, ds_ref, up, down, side, cup, cdown, ws_ref, t_ref, stats_ref, gb_ref,
    e_ref, msg_ref, padded_ref, *, index,
):
    rows, cols, cell, middle = ds_ref.shape
    width = e_ref.shape[1]
    fill_padded(place_ref, padded_ref, ds_ref, (up, down, side, cup, cdown))
    mean, rstd = stats_ref[0:1, :], stats_ref[1:2, :]
    gain, bias = gb_ref[2 * index : 2 * index + 1, :width], gb_ref[2 * index + 1 : 2 * index + 2, :width]

    def one_row(r, carry):
        grad = spatial_back(padded_ref, ws_ref, r, cols, cell, width)
        e_ref[block_rows(r, cols * cell), :] = grad
        return carry

    lax.fori_loop(0, rows, one_row, 0)

    def one_cell(c, carry):
        bias_sum, gain_sum = carry
        normal = (t_ref[cell_rows(c), :] - mean) * rstd
        value = normal * gain + bias
        sigma = sigmoid(value)
        e = e_ref[cell_rows(c), :] * valid_ref[c] * (sigma * (1.0 + value * (1.0 - sigma)))
        e_ref[cell_rows(c), :] = e
        return (bias_sum + fold8(e), gain_sum + fold8(e * normal))

    start = jnp.zeros((8, width), F32)
    bias_sum, gain_sum = lax.fori_loop(0, rows * cols, one_cell, (start, start))
    send_sums(bias_sum, gain_sum, msg_ref)


def input_grad_kernel(
    place_ref, valid_ref, ds_ref, up, down, side, cup, cdown, ws_ref, dpre_ref, out_ref, padded_ref
):
    rows, cols, cell, middle = ds_ref.shape
    width = out_ref.shape[1]
    fill_padded(place_ref, padded_ref, ds_ref, (up, down, side, cup, cdown))

    def one_row(r, carry):
        grad = spatial_back(padded_ref, ws_ref, r, cols, cell, width)
        for c in range(cols):
            rows_of = cell_rows(r * cols + c)
            out_ref[rows_of, :] = (grad[c * cell : (c + 1) * cell] + dpre_ref[rows_of, :]) * valid_ref[
                r * cols + c
            ]
        return carry

    lax.fori_loop(0, rows, one_row, 0)


def temporal_kernel(
    valid_ref, s_ref, msg_ref, gb_ref, wt_ref, columns_ref, t_ref, stats_ref, out_ref, *, index
):
    rows, middle = s_ref.shape
    mean, rstd, count = receive_stats(msg_ref)
    keep_stats(stats_ref, mean, rstd, count)
    gain, bias = gb_ref[2 * index : 2 * index + 1, :], gb_ref[2 * index + 1 : 2 * index + 2, :]

    def one_cell(c, _):
        value = (s_ref[cell_rows(c), :] - mean) * rstd * gain + bias
        inner = value * sigmoid(value) * valid_ref[c]
        columns_ref[cell_rows(c), 0:middle] = earlier_frame(inner).astype(BF16)
        columns_ref[cell_rows(c), middle : 2 * middle] = inner.astype(BF16)
        columns_ref[cell_rows(c), 2 * middle : 3 * middle] = later_frame(inner).astype(BF16)
        return 0

    lax.fori_loop(0, rows // CELL, one_cell, 0)

    def one_block(i, _):
        t_ref[block_rows(i, 320), :] = jnp.dot(
            columns_ref[block_rows(i, 320), :], wt_ref[...], preferred_element_type=F32
        )
        return 0

    lax.fori_loop(0, rows // 320, one_block, 0)
    send_stats(t_ref, valid_ref, out_ref)


def middle_kernel(
    place_ref, valid_ref, t_ref, msg_ref, gb_ref, stats_ref, tile_ref, top, bottom, side, ctop, cbottom,
    *, index,
):
    width = t_ref.shape[1]
    rows, cols = tile_ref.shape[:2]
    mean, rstd, count = receive_stats(msg_ref)
    keep_stats(stats_ref, mean, rstd, count)
    gain, bias = gb_ref[2 * index : 2 * index + 1, :width], gb_ref[2 * index + 1 : 2 * index + 2, :width]
    for r in range(rows):
        for c in range(cols):
            number = r * cols + c
            value = (t_ref[number * CELL : (number + 1) * CELL, :] - mean) * rstd * gain + bias
            tile_ref[r, c] = (value * sigmoid(value) * valid_ref[number]).astype(BF16)
    write_edges(place_ref, tile_ref, (top, bottom, side, ctop, cbottom))


def top_kernel(
    valid_ref, t_ref, msg_ref, gb_ref, x_ref, cot_ref, stats_ref, out_ref, dpre_ref, msg_out, *, index
):
    rows, width = t_ref.shape
    mean, rstd, count = receive_stats(msg_ref)
    keep_stats(stats_ref, mean, rstd, count)
    gain, bias = gb_ref[2 * index : 2 * index + 1, :width], gb_ref[2 * index + 1 : 2 * index + 2, :width]

    def one_cell(c, carry):
        bias_sum, gain_sum = carry
        normal = (t_ref[cell_rows(c), :] - mean) * rstd
        pre = normal * gain + bias + x_ref[cell_rows(c), :].astype(F32)
        sigma = sigmoid(pre)
        valid = valid_ref[c]
        out_ref[cell_rows(c), :] = pre * sigma * valid
        dpre = cot_ref[cell_rows(c), :].astype(F32) * valid * (sigma * (1.0 + pre * (1.0 - sigma)))
        dpre_ref[cell_rows(c), :] = dpre
        return (bias_sum + fold8(dpre), gain_sum + fold8(dpre * normal))

    start = jnp.zeros((8, width), F32)
    bias_sum, gain_sum = lax.fori_loop(0, rows // CELL, one_cell, (start, start))
    send_sums(bias_sum, gain_sum, msg_out)


def temporal_grad_kernel(
    valid_ref, e_ref, t_ref, tstats_ref, msg_ref, s_ref, sstats_ref, gb_ref, wt_ref,
    dt_ref, en_ref, sums_ref, msg_out, columns_ref, *, index,
):
    rows, width = e_ref.shape
    middle = s_ref.shape[1]
    bias_grad, gain_grad = receive_sums(msg_ref)
    sums_ref[0:1, :] = gain_grad
    sums_ref[1:2, :] = bias_grad
    mean, rstd, count = tstats_ref[0:1, :], tstats_ref[1:2, :], tstats_ref[2:3, :]
    gain = gb_ref[2 * index + 2 : 2 * index + 3, :width]

    def one_cell(c, _):
        normal = (t_ref[cell_rows(c), :] - mean) * rstd
        dt = (rstd * gain) * (
            e_ref[cell_rows(c), :] - valid_ref[c] * ((bias_grad + normal * gain_grad) / count)
        )
        dt_ref[cell_rows(c), :] = dt.astype(BF16)
        columns_ref[cell_rows(c), 0:width] = later_frame(dt).astype(BF16)
        columns_ref[cell_rows(c), width : 2 * width] = dt.astype(BF16)
        columns_ref[cell_rows(c), 2 * width : 3 * width] = earlier_frame(dt).astype(BF16)
        return 0

    lax.fori_loop(0, rows // CELL, one_cell, 0)

    def one_block(i, _):
        total = None
        for tap in range(3):
            term = lax.dot_general(
                columns_ref[block_rows(i, 320), tap * width : (tap + 1) * width],
                wt_ref[tap * middle : (tap + 1) * middle, :],
                (((1,), (1,)), ((), ())),
                preferred_element_type=F32,
            )
            total = term if total is None else total + term
        en_ref[block_rows(i, 320), :] = total
        return 0

    lax.fori_loop(0, rows // 320, one_block, 0)
    mean_s, rstd_s = sstats_ref[0:1, :], sstats_ref[1:2, :]
    gain_s, bias_s = gb_ref[2 * index : 2 * index + 1, :], gb_ref[2 * index + 1 : 2 * index + 2, :]

    def one_mid_cell(c, carry):
        bias_sum, gain_sum = carry
        normal = (s_ref[cell_rows(c), :] - mean_s) * rstd_s
        value = normal * gain_s + bias_s
        sigma = sigmoid(value)
        e = en_ref[cell_rows(c), :] * valid_ref[c] * (sigma * (1.0 + value * (1.0 - sigma)))
        en_ref[cell_rows(c), :] = e
        return (bias_sum + fold8(e), gain_sum + fold8(e * normal))

    start = jnp.zeros((8, middle), F32)
    bias_sum, gain_sum = lax.fori_loop(0, rows // CELL, one_mid_cell, (start, start))
    send_sums(bias_sum, gain_sum, msg_out)


def temporal_weight_kernel(columns_ref, dt_ref, grad_ref):
    middle = columns_ref.shape[1] // 3
    for tap in range(3):
        grad_ref[tap * middle : (tap + 1) * middle, :] = lax.dot_general(
            columns_ref[:, tap * middle : (tap + 1) * middle],
            dt_ref[...],
            (((0,), (0,)), ((), ())),
            preferred_element_type=F32,
        )


def ds_kernel(
    place_ref, valid_ref, en_ref, s_ref, stats_ref, msg_ref, gb_ref,
    sums_ref, tile_ref, top, bottom, side, ctop, cbottom, *, index,
):
    rows, cols = tile_ref.shape[:2]
    bias_grad, gain_grad = receive_sums(msg_ref)
    sums_ref[0:1, :] = gain_grad
    sums_ref[1:2, :] = bias_grad
    mean, rstd, count = stats_ref[0:1, :], stats_ref[1:2, :], stats_ref[2:3, :]
    scale = rstd * gb_ref[2 * index : 2 * index + 1, :]
    for r in range(rows):
        for c in range(cols):
            number = r * cols + c
            block = slice(number * CELL, (number + 1) * CELL)
            normal = (s_ref[block, :] - mean) * rstd
            tile_ref[r, c] = (
                scale
                * (en_ref[block, :] - valid_ref[number] * ((bias_grad + normal * gain_grad) / count))
            ).astype(BF16)
    write_edges(place_ref, tile_ref, (top, bottom, side, ctop, cbottom))


def run(kernel, ins, outs, scratch=(), scalars=0, **settings):
    return pl.pallas_call(
        functools.partial(kernel, **settings),
        out_shape=[jax.ShapeDtypeStruct(shape, dtype) for shape, dtype in outs],
        in_specs=[SMEM] * scalars + [VMEM] * (len(ins) - scalars),
        out_specs=[VMEM] * len(outs),
        scratch_shapes=list(scratch),
        compiler_params=pltpu.CompilerParams(vmem_limit_bytes=56 * 2**20),
    )(*ins)


def slot_of_pieces(owner_list, slot_count, device_total):
    owner_ids = owner_list[:, 0]
    onehot = (owner_ids[:, None] == jnp.arange(device_total, dtype=jnp.int32)[None, :]).astype(
        jnp.int32
    )
    earlier = jnp.cumsum(onehot, axis=0) - onehot
    ranking = jnp.sum(earlier * onehot, axis=1)
    return owner_ids * slot_count + ranking


def exchange(message):
    return lax.all_to_all(message, AXES, 0, 0, tiled=True)


def swap_edges(edges):
    top, bottom, side, corner_top, corner_bottom = edges
    count = lax.axis_size("ha")
    cores = lax.axis_size("wa")
    forward = [(i, i + 1) for i in range(count - 1)]
    backward = [(i + 1, i) for i in range(count - 1)]
    across = [(0, 1), (1, 0)]

    def both(moves):
        return [(a * cores + i, b * cores + j) for a, b in moves for i, j in across]

    up = lax.ppermute(bottom, "ha", forward)
    down = lax.ppermute(top, "ha", backward)
    corner_up = lax.ppermute(corner_bottom, ("ha", "wa"), both(forward))
    corner_down = lax.ppermute(corner_top, ("ha", "wa"), both(backward))
    beside = lax.ppermute(side, "wa", across)
    return [up, down, beside, corner_up, corner_down]


def per_device(
    block_input,
    cotangent,
    frame_sides,
    owner_list,
    master_slots,
    first_slots,
    second_slots,
    norm_gains,
    norm_biases,
    norm_first,
    norm_second,
):
    clip_count, frames, tile_rows, tile_cols, width = block_input.shape
    devices = lax.axis_size(AXES)
    slot_count, piece_len = master_slots.shape
    middle = norm_gains.shape[0] // 2 - width
    middle_pad = -(-middle // LANES) * LANES
    rows = clip_count * frames * tile_rows * tile_cols

    low_slots = master_slots.astype(BF16).reshape(slot_count * PIECE_ROWS, LANES)
    all_weights = lax.all_gather(low_slots, AXES, axis=0, tiled=True)

    own_side = frame_sides[0]
    row_ids = lax.axis_index("ha") * tile_rows + jnp.arange(tile_rows, dtype=jnp.int32)
    col_ids = lax.axis_index("wa") * tile_cols + jnp.arange(tile_cols, dtype=jnp.int32)
    grid_rows = tile_rows * lax.axis_size("ha")
    grid_cols = tile_cols * lax.axis_size("wa")
    valid = (
        (row_ids[:, None] >= grid_rows - own_side) & (col_ids[None, :] >= grid_cols - own_side)
    ).astype(F32)
    valid_flat = valid.reshape(-1)
    place = lax.axis_index("wa").reshape(1)
    slot_index = slot_of_pieces(owner_list, slot_count, devices)
    batches, heights, cores = (lax.axis_size(axis) for axis in AXES)
    owner, ranking = slot_index // slot_count, slot_index % slot_count
    turned = (owner % cores * heights + owner // cores % heights) * batches + owner // (cores * heights)
    grad_slots = turned * slot_count + ranking

    bounds = [0, middle, middle + width, 2 * middle + width, 2 * middle + 2 * width]
    gb = []
    for i in range(4):
        for vector in (norm_gains, norm_biases):
            part = vector[bounds[i] : bounds[i + 1]]
            gb.append(jnp.pad(part, (0, middle_pad - part.shape[0])))
    gb = jnp.stack(gb)

    def to_tile(array):
        return jnp.transpose(array, (2, 3, 1, 0, 4)).reshape(tile_rows, tile_cols, CELL, width)

    x_tile = to_tile(block_input) * valid[:, :, None, None].astype(BF16)
    cot_tile = to_tile(cotangent)
    edge = jnp.where(place[0] == 0, tile_cols - 1, 0)
    x_side = lax.dynamic_index_in_dim(x_tile, edge, axis=1, keepdims=False)
    x_halo = swap_edges([x_tile[0], x_tile[-1], x_side, x_side[0], x_side[-1]])

    tap_rows = 9 * width
    stage = [pltpu.VMEM((144, LANES), F32), pltpu.VMEM((5, 32, LANES), F32)]
    half = tap_rows * middle // piece_len + 3 * middle * width // piece_len
    weight_shapes = [((tap_rows, middle_pad), BF16), ((3 * middle_pad, width), BF16)]
    weights = []
    for unit in range(2):
        weights.append(
            run(unpack_weights_kernel, [slot_index, all_weights], weight_shapes, stage, 1, base=unit * half)
        )

    tile_shape = (tile_rows, tile_cols, CELL, width)
    mid_tile = (tile_rows, tile_cols, CELL, middle_pad)
    padded_tile = (tile_rows + 2, tile_cols + 2, CELL, width)
    padded_mid = (tile_rows + 2, tile_cols + 2, CELL, middle_pad)
    stats_mid = (devices, 1, 2 * middle_pad + LANES)
    stats_wide = (devices, 1, 2 * width + LANES)

    def edge_shapes(lanes):
        row, col = (tile_cols, CELL, lanes), (tile_rows, CELL, lanes)
        return [(row, BF16), (row, BF16), (col, BF16), ((CELL, lanes), BF16), ((CELL, lanes), BF16)]

    def unit_forward(tile, halo, ws, wt, index):
        padded, s, msg = run(
            spatial_kernel,
            [place, valid_flat, tile, *halo, ws],
            [(padded_tile, BF16), ((rows, middle_pad), F32), (stats_mid, F32)],
            scalars=2,
        )
        columns, t, s_stats, msg = run(
            temporal_kernel,
            [valid_flat, s, exchange(msg), gb, wt],
            [
                ((rows, 3 * middle_pad), BF16),
                ((rows, width), F32),
                ((8, middle_pad), F32),
                (stats_wide, F32),
            ],
            scalars=1,
            index=index,
        )
        return padded, s, s_stats, columns, t, exchange(msg)

    (ws1, wt1), (ws2, wt2) = weights
    padded1, s1, s_stats1, columns1, t1, msg = unit_forward(x_tile, x_halo, ws1, wt1, 0)
    t_stats1, y_tile, *edges = run(
        middle_kernel,
        [place, valid_flat, t1, msg, gb],
        [((8, width), F32), (tile_shape, BF16)] + edge_shapes(width),
        scalars=2,
        index=1,
    )
    padded2, s2, s_stats2, columns2, t2, msg = unit_forward(y_tile, swap_edges(edges), ws2, wt2, 2)
    t_stats2, block_output, dpre, msg = run(
        top_kernel,
        [valid_flat, t2, msg, gb, x_tile.reshape(rows, width), cot_tile.reshape(rows, width)],
        [((8, width), F32), ((rows, width), F32), ((rows, width), F32), ((devices, 1, 2 * width), F32)],
        scalars=1,
        index=3,
    )

    def unit_backward(e, msg, t, t_stats, s, s_stats, columns, padded, wt, index):
        dt, en, t_sums, msg = run(
            temporal_grad_kernel,
            [valid_flat, e, t, t_stats, exchange(msg), s, s_stats, gb, wt],
            [
                ((rows, width), BF16),
                ((rows, middle_pad), F32),
                ((2, width), F32),
                ((devices, 1, 2 * middle_pad), F32),
            ],
            [pltpu.VMEM((rows, 3 * width), BF16)],
            scalars=1,
            index=index,
        )
        s_sums, ds, *edges = run(
            ds_kernel,
            [place, valid_flat, en, s, s_stats, exchange(msg), gb],
            [((2, middle_pad), F32), (mid_tile, BF16)] + edge_shapes(middle_pad),
            scalars=2,
            index=index,
        )
        halo = swap_edges(edges)
        (wt_grad,) = run(temporal_weight_kernel, [columns, dt], [((3 * middle_pad, width), F32)])
        (ws_grad,) = run(spatial_weight_kernel, [padded, ds], [((tap_rows, middle_pad), F32)])
        return ds, halo, ws_grad, wt_grad, s_sums, t_sums

    ds, halo, ws_grad2, wt_grad2, s_sums2, t_sums2 = unit_backward(
        dpre, msg, t2, t_stats2, s2, s_stats2, columns2, padded2, wt2, 2
    )
    e1, msg = run(
        spatial_grad_kernel,
        [place, valid_flat, ds, *halo, ws2, t1, t_stats1, gb],
        [((rows, width), F32), ((devices, 1, 2 * width), F32)],
        [pltpu.VMEM(padded_mid, BF16)],
        scalars=2,
        index=1,
    )
    ds, halo, ws_grad1, wt_grad1, s_sums1, t_sums1 = unit_backward(
        e1, msg, t1, t_stats1, s1, s_stats1, columns1, padded1, wt1, 0
    )
    (packed,) = run(
        pack_grads_kernel,
        [grad_slots, ws_grad1, wt_grad1, ws_grad2, wt_grad2],
        [((devices * slot_count * PIECE_ROWS, LANES), BF16)],
        stage,
        scalars=1,
    )
    grad_mine = packed
    for axis in ("wa", "ha", "batch"):
        grad_mine = lax.psum_scatter(grad_mine, axis, scatter_dimension=0, tiled=True)
    (input_grad,) = run(
        input_grad_kernel,
        [place, valid_flat, ds, *halo, ws1, dpre],
        [((rows, width), F32)],
        [pltpu.VMEM(padded_mid, BF16)],
        scalars=2,
    )

    def from_tile(array):
        array = array.reshape(tile_rows, tile_cols, frames, clip_count, width)
        return jnp.transpose(array, (3, 2, 0, 1, 4))

    grad_mine = grad_mine.astype(F32).reshape(slot_count, piece_len)
    correction = 1.0 - 0.5**STEP
    step_rate = 1.8 / math.sqrt(9.0 * width)
    first_new = 0.5 * first_slots + 0.5 * grad_mine
    second_new = 0.5 * second_slots + 0.5 * grad_mine * grad_mine
    master_new = master_slots - step_rate * (
        first_new / correction / (jnp.sqrt(second_new / correction) + ADAM_EPSILON)
        + DECAY_RATE * master_slots
    )
    weight_copy = master_new.astype(BF16)
    norm_grad = jnp.concatenate([s_sums1[:, :middle], t_sums1, s_sums2[:, :middle], t_sums2], axis=1)
    norm_pair = jnp.stack([norm_gains, norm_biases])
    norm_first_new = 0.5 * norm_first + 0.5 * norm_grad
    norm_second_new = 0.5 * norm_second + 0.5 * norm_grad * norm_grad
    norm_new = norm_pair - NORM_RATE * (norm_first_new / correction) / (
        jnp.sqrt(norm_second_new / correction) + ADAM_EPSILON
    )
    return (
        from_tile(block_output),
        from_tile(input_grad),
        master_new,
        first_new,
        second_new,
        weight_copy,
        norm_first_new,
        norm_second_new,
        norm_new,
    )


def solution(mesh):
    wide = P("batch", None, "ha", "wa", None)
    owned = P(AXES, None)
    return jax.shard_map(
        per_device,
        mesh=mesh,
        in_specs=(wide, wide, P("batch"), P(), owned, owned, owned, P(), P(), P(), P()),
        out_specs=(wide, wide, owned, owned, owned, owned, P(), P(), P()),
        check_vma=False,
    )
```

time: 1220 us -> 492 us (0.40); the launches traced: 1210 us -> 490 us
  blocking collectives: 647 us -> 44 us
  local copies, waits for them, and re-layouts: 274 us -> 15.1 us
  Pallas kernels: 0 us -> 165 us
  waiting for transfers between devices: 40.4 us -> 179 us
  matrix products: 98.9 us -> 0 us
  other arithmetic: 78 us -> 15.3 us
    psum x12 -> x0, blocking collectives: 480 us -> none  [the longest x4 161 us: norm_forward(): lax.psum(jnp.sum(centered * centered, axis=(0, 1, 2, 3)), ('batch', 'ha',...]
    unnamed x2 -> x0, blocking collectives: 167 us -> none
    pallas_call x0 -> x19, Pallas kernels: none -> 165 us  [run(): pl.pallas_call(functools.partial(kernel, **settings), out_shape=[jax.Shap...]
    dot_general x12 -> x0, matrix products: 98.9 us -> none  [the longest x2 44.5 us: unit_backward(): jnp.einsum('rkc,kic->ri', back_a, spatial_w.reshape(9, model_width, middl...]
    another operation x12 -> x11, local copies, waits for them, and re-layouts: 84 us -> 0.81 us  [the longest x9 0.67 us: per_device(): gb = jnp.stack(gb)]
    concatenate x12 -> x1, local copies, waits for them, and re-layouts: 73 us -> 0.1 us  [per_device(): jnp.concatenate([s_sums1[:, :middle], t_sums1, s_sums2[:, :middle], t_sum...]
    reduce_scatter x0 -> x3, waiting for transfers between devices: none -> 69.3 us  [per_device(): lax.psum_scatter(grad_mine, axis, scatter_dimension=0, tiled=True)]
    all_to_all x0 -> x4, blocking collectives: none -> 44 us  [exchange(): return lax.all_to_all(message, AXES, 0, 0, tiled=True)]
  transfers between devices with their start and end apart: 18 -> 28, of which waited for: 4 -> 10; matrix products, arithmetic and copies ran while one was open for 24% -> 4% of each run, Pallas kernels for 0% -> 11%
where the time goes in v1:
time: 492 us; the launch traced here: 490 us
  waiting for transfers between devices  179 us (36%)
  Pallas kernels  165 us (34%)
  starting transfers between devices  56.6 us (12%)
  blocking collectives  44 us (9%)
  other arithmetic  15.3 us (3%)
  between operations  15.3 us (3%)
  local copies, waits for them, and re-layouts  15.1 us (3%)
    pallas_call x19, Pallas kernels, run(): pl.pallas_call(functools.partial(kernel, **settings), out_shape=[jax.Shap...  165 us
    reduce_scatter x3, waiting for transfers between devices, per_device(): lax.psum_scatter(grad_mine, axis, scatter_dimension=0, tiled=True)  69.3 us
    all_gather x1, waiting for transfers between devices, per_device(): all_weights = lax.all_gather(low_slots, AXES, axis=0, tiled=True)  54.2 us
    all_to_all x4, blocking collectives, exchange(): return lax.all_to_all(message, AXES, 0, 0, tiled=True)  44 us
    all_to_all x4, waiting for transfers between devices, exchange(): return lax.all_to_all(message, AXES, 0, 0, tiled=True)  22 us
    ppermute x4, starting transfers between devices, swap_edges(): corner_up = lax.ppermute(corner_bottom, ('ha', 'wa'), both(forward))  16.9 us
    ppermute x4, starting transfers between devices, swap_edges(): up = lax.ppermute(bottom, 'ha', forward)  14.1 us
    all_to_all x4, starting transfers between devices, exchange(): return lax.all_to_all(message, AXES, 0, 0, tiled=True)  13.4 us
  transfers between devices with their start and end apart: 28, of which 10 were waited for; matrix products, arithmetic and copies ran while one was open for 4% of the time, Pallas kernels for 11%

profile of v1, /device:TPU:0, one launch (start us, length us, event | category | flops | bytes accessed | tf_op | source)
XLA Modules:
  0.0 490.4 jit_solution(7594645859366525638)
XLA Ops:
  12.5 4.9 %collective-permute-start.3 = (bf16[64,256]{1,0:T(8,128)(2,1)S(1)}, bf16[64,256]{1,0:T(8,128)(2,1)S(1)}, u32[]{:S(2)}, u32[]{:S(2)}) collective-permute-start(bf16[64,256]{1,0:T(8,128)(2,1)S(1)} %get-tuple-element.125), channel_id=1, source_target_pairs={{0,3},{1,2},{2,5},{3,4},{4,7},{5,6},{8,11},{9,10},{10,13},{11,12},... | collective-permute-start | bytes 98312 | tf_op jit(solution)/shard_map/ppermute | solution.py:555
  19.5 5.1 %collective-permute-start = (bf16[5,64,256]{2,1,0:T(8,128)(2,1)S(1)}, bf16[5,64,256]{2,1,0:T(8,128)(2,1)S(1)}, u32[]{:S(2)}, u32[]{:S(2)}) collective-permute-start(bf16[5,64,256]{2,1,0:T(8,128)(2,1)S(1)} %get-tuple-element.127), channel_id=1, source_target_pairs={{0,2},{2,4},{4,6},{1,3},{3,5},{5,7},{8,10},{10,12},{12,14},{9,11},... | collective-permute-start | bytes 491528 | tf_op jit(solution)/shard_map/ppermute | solution.py:553
  24.8 9.1 %reduce-window.6 = s32[32,14,128]{2,1,0:T(8,128)S(1)} reduce-window(s32[32,14,128]{2,1,0:T(8,128)S(1)} %reshape.122, s32[]{:T(128)} %constant.99.clone.1), window={size=1x1x128 pad=0_0x0_0x127_0}, to_apply=%region_0.0 | reduce-window | flops 7282688 | bytes 458756 | tf_op jit(solution)/shard_map/reduce-window
  36.1 54.2 %all-gather.2.cloned.1.call-done.all_ref = bf16[28160,128]{1,0:T(8,128)(2,1)} async-done(((bf16[880,128]{1,0:T(8,128)(2,1)}), bf16[28160,128]{1,0:T(8,128)(2,1)}) %all-gather.2.cloned.1.call-update) | async-done | bytes 7208976 | tf_op jit(solution)/shard_map/all_gather | solution.py:582
  90.3 13.9 %shard_map.178 = (bf16[2304,640]{1,0:T(8,128)(2,1)}, bf16[1920,256]{1,0:T(8,128)(2,1)}) custom-call(s32[1728]{0:T(1024)} %get-tuple-element.123.slot_ref, bf16[28160,128]{1,0:T(8,128)(2,1)} %all-gather.2.cloned.1.call-done.all_ref), custom_call_target="tpu_custom_call" | custom-call | tf_op jit(solution)/shard_map/pallas_call | solution.py:518
  105.0 8.7 %shard_map.179 = (bf16[5,7,64,256]{3,2,1,0:T(8,128)(2,1)}, f32[960,640]{1,0:T(8,128)}, f32[32,1,1408]{2,1,0:T(1,128)}) custom-call(s32[1]{0:T(128)} %bitcast.2.place_ref, f32[15]{0:T(128)} %reshape.121.valid_ref, bf16[3,5,64,256]{3,2,1,0:T(8,128)(2,1)} %copy-done, bf16[5,64,256]{2,1,0:T(8,128)(2,1)} %copy-done.18, bf16[5,64,256]{2,1,0:T(8,128)(2,1)} %copy-done.17, ...), custom_call_target="tpu_custom_call" | custom-call | tf_op jit(solution)/shard_map/pallas_call | solution.py:518
  117.7 7.9 %all-to-all-done.msg_ref = f32[32,1,1408]{2,1,0:T(1,128)S(1)} async-done(((f32[32,1,1408]{2,1,0:T(1,128)}), f32[32,1,1408]{2,1,0:T(1,128)S(1)}, u32[]{:S(2)}, u32[]{:S(2)}) %all-to-all-start) | async-done | bytes 180256 | tf_op jit(solution)/shard_map/all_to_all | solution.py:539
  126.2 7.8 %shard_map.180 = (bf16[960,1920]{1,0:T(8,128)(2,1)}, f32[960,256]{1,0:T(8,128)}, f32[8,640]{1,0:T(8,128)}, f32[32,1,640]{2,1,0:T(1,128)}) custom-call(f32[15]{0:T(128)} %reshape.121.valid_ref, f32[960,640]{1,0:T(8,128)} %get-tuple-element.63.s_ref, f32[32,1,1408]{2,1,0:T(1,128)} %copy-done.4, f32[8,640]{1,0:T(8,128)} %stack.44.gb_ref, ...), custom_call_target="tpu_custom_call" | custom-call | tf_op jit(solution)/shard_map/pallas_call | solution.py:518
  134.0 10.9 %all_to_all.40.msg_ref = f32[32,1,640]{2,1,0:T(1,128)} all-to-all(f32[32,1,640]{2,1,0:T(1,128)} %get-tuple-element.67), channel_id=1, replica_groups=mesh['batch'=4,'ha'=4,'wa'=2] {'batch','ha','wa'}, dimensions={0} | all-to-all | bytes 163840 | tf_op jit(solution)/shard_map/all_to_all | solution.py:539
  157.4 14.0 %shard_map.182 = (bf16[2304,640]{1,0:T(8,128)(2,1)}, bf16[1920,256]{1,0:T(8,128)(2,1)}) custom-call(s32[1728]{0:T(1024)} %get-tuple-element.123.slot_ref, bf16[28160,128]{1,0:T(8,128)(2,1)} %all-gather.2.cloned.1.call-done.all_ref), custom_call_target="tpu_custom_call" | custom-call | tf_op jit(solution)/shard_map/pallas_call | solution.py:518
  172.1 8.8 %shard_map.183 = (bf16[5,7,64,256]{3,2,1,0:T(8,128)(2,1)}, f32[960,640]{1,0:T(8,128)}, f32[32,1,1408]{2,1,0:T(1,128)}) custom-call(s32[1]{0:T(128)} %bitcast.2.place_ref, f32[15]{0:T(128)} %reshape.121.valid_ref, bf16[3,5,64,256]{3,2,1,0:T(8,128)(2,1)} %get-tuple-element.68.tile_ref, bf16[5,64,256]{2,1,0:T(8,128)(2,1)} %copy-done.19, ...), custom_call_target="tpu_custom_call" | custom-call | tf_op jit(solution)/shard_map/pallas_call | solution.py:518
  180.9 5.1 %all-to-all-start.2 = ((f32[32,1,1408]{2,1,0:T(1,128)}), f32[32,1,1408]{2,1,0:T(1,128)S(1)}, u32[]{:S(2)}, u32[]{:S(2)}) async-start(f32[32,1,1408]{2,1,0:T(1,128)} %get-tuple-element.76), calls=%async_computation.2 | async-start | bytes 360448 | tf_op jit(solution)/shard_map/all_to_all | solution.py:539
  187.2 7.5 %all-to-all-done.2.msg_ref = f32[32,1,1408]{2,1,0:T(1,128)S(1)} async-done(((f32[32,1,1408]{2,1,0:T(1,128)}), f32[32,1,1408]{2,1,0:T(1,128)S(1)}, u32[]{:S(2)}, u32[]{:S(2)}) %all-to-all-start.2) | async-done | bytes 180256 | tf_op jit(solution)/shard_map/all_to_all | solution.py:539
  195.4 7.8 %shard_map.184 = (bf16[960,1920]{1,0:T(8,128)(2,1)}, f32[960,256]{1,0:T(8,128)}, f32[8,640]{1,0:T(8,128)}, f32[32,1,640]{2,1,0:T(1,128)}) custom-call(f32[15]{0:T(128)} %reshape.121.valid_ref, f32[960,640]{1,0:T(8,128)} %get-tuple-element.75.s_ref, f32[32,1,1408]{2,1,0:T(1,128)} %copy-done.5, f32[8,640]{1,0:T(8,128)} %stack.44.gb_ref, ...), custom_call_target="tpu_custom_call" | custom-call | tf_op jit(solution)/shard_map/pallas_call | solution.py:518
  206.7 6.6 %all-to-all-done.3.msg_ref = f32[32,1,640]{2,1,0:T(1,128)S(1)} async-done(((f32[32,1,640]{2,1,0:T(1,128)}), f32[32,1,640]{2,1,0:T(1,128)S(1)}, u32[]{:S(2)}, u32[]{:S(2)}) %all-to-all-start.3) | async-done | bytes 81952 | tf_op jit(solution)/shard_map/all_to_all | solution.py:539
  217.9 10.7 %all_to_all.41.msg_ref = f32[32,1,512]{2,1,0:T(1,128)} all-to-all(f32[32,1,512]{2,1,0:T(1,128)} %get-tuple-element.83), channel_id=1, replica_groups=mesh['batch'=4,'ha'=4,'wa'=2] {'batch','ha','wa'}, dimensions={0} | all-to-all | bytes 131072 | tf_op jit(solution)/shard_map/all_to_all | solution.py:539
  228.6 8.1 %shard_map.186 = (bf16[960,256]{1,0:T(8,128)(2,1)}, f32[960,640]{1,0:T(8,128)}, f32[2,256]{1,0:T(2,128)}, f32[32,1,1280]{2,1,0:T(1,128)}) custom-call(f32[15]{0:T(128)} %reshape.121.valid_ref, f32[960,256]{1,0:T(8,128)} %get-tuple-element.81.e_ref.dpre_ref, f32[960,256]{1,0:T(8,128)} %get-tuple-element.78.t_ref, f32[8,256]{1,0:T(8,128)} %get-tuple-element.82.tstats_ref, ...), custom_call_target="tpu_custom_call" | custom-call | tf_op jit(solution)/shard_map/pallas_call | solution.py:518
  236.7 11.8 %all_to_all.42.msg_ref = f32[32,1,1280]{2,1,0:T(1,128)} all-to-all(f32[32,1,1280]{2,1,0:T(1,128)} %get-tuple-element.86), channel_id=1, replica_groups=mesh['batch'=4,'ha'=4,'wa'=2] {'batch','ha','wa'}, dimensions={0} | all-to-all | bytes 327680 | tf_op jit(solution)/shard_map/all_to_all | solution.py:539
  248.5 4.7 shard_map.187
  266.8 10.8 %collective-permute-done.14.cdown = bf16[64,640]{1,0:T(8,128)(2,1)S(1)} collective-permute-done((bf16[64,640]{1,0:T(8,128)(2,1)}, bf16[64,640]{1,0:T(8,128)(2,1)S(1)}, u32[]{:S(2)}, u32[]{:S(2)}) %collective-permute-start.14) | collective-permute-done | bytes 81952 | tf_op jit(solution)/shard_map/ppermute | solution.py:556
  278.6 9.0 %shard_map.188 = (f32[960,256]{1,0:T(8,128)}, f32[32,1,512]{2,1,0:T(1,128)}) custom-call(s32[1]{0:T(128)} %bitcast.2.place_ref, f32[15]{0:T(128)} %reshape.121.valid_ref, bf16[3,5,64,640]{3,2,1,0:T(8,128)(2,1)} %get-tuple-element.87.ds_ref, bf16[5,64,640]{2,1,0:T(8,128)(2,1)} %copy-done.10, bf16[5,64,640]{2,1,0:T(8,128)(2,1)} %copy-done.11, ...), custom_call_target="tpu_custom_call" | custom-call | tf_op jit(solution)/shard_map/pallas_call | solution.py:518
  287.5 10.6 %all_to_all.43.msg_ref = f32[32,1,512]{2,1,0:T(1,128)} all-to-all(f32[32,1,512]{2,1,0:T(1,128)} %get-tuple-element.95), channel_id=1, replica_groups=mesh['batch'=4,'ha'=4,'wa'=2] {'batch','ha','wa'}, dimensions={0} | all-to-all | bytes 131072 | tf_op jit(solution)/shard_map/all_to_all | solution.py:539
  298.2 8.1 %shard_map.189 = (bf16[960,256]{1,0:T(8,128)(2,1)}, f32[960,640]{1,0:T(8,128)}, f32[2,256]{1,0:T(2,128)}, f32[32,1,1280]{2,1,0:T(1,128)}) custom-call(f32[15]{0:T(128)} %reshape.121.valid_ref, f32[960,256]{1,0:T(8,128)} %get-tuple-element.94.e_ref, f32[960,256]{1,0:T(8,128)} %get-tuple-element.66.t_ref, f32[8,256]{1,0:T(8,128)} %get-tuple-element.93.stats_ref.tstats_ref, ...), custom_call_target="tpu_custom_call" | custom-call | tf_op jit(solution)/shard_map/pallas_call | solution.py:518
  313.6 8.1 %shard_map.194.ws2_ref = f32[2304,640]{1,0:T(8,128)} custom-call(bf16[5,7,64,256]{3,2,1,0:T(8,128)(2,1)} %get-tuple-element.108.padded_ref, bf16[3,5,64,640]{3,2,1,0:T(8,128)(2,1)} %get-tuple-element.87.ds_ref), custom_call_target="tpu_custom_call" | custom-call | tf_op jit(solution)/shard_map/pallas_call | solution.py:518
  327.0 4.7 shard_map.190
  331.8 8.0 %shard_map.192.ws_ref = f32[2304,640]{1,0:T(8,128)} custom-call(bf16[5,7,64,256]{3,2,1,0:T(8,128)(2,1)} %get-tuple-element.105.padded_ref, bf16[3,5,64,640]{3,2,1,0:T(8,128)(2,1)} %get-tuple-element.99.ds_ref), custom_call_target="tpu_custom_call" | custom-call | tf_op jit(solution)/shard_map/pallas_call | solution.py:518
  339.8 29.5 %shard_map.196 = bf16[28160,128]{1,0:T(8,128)(2,1)} custom-call(s32[1728]{0:T(1024)} %get-tuple-element.122.slot_ref, f32[2304,640]{1,0:T(8,128)} %shard_map.192.ws_ref, f32[1920,256]{1,0:T(8,128)} %shard_map.193.wt_ref, f32[2304,640]{1,0:T(8,128)} %shard_map.194.ws2_ref, f32[1920,256]{1,0:T(8,128)} %shard_map.195.wt2_ref), custom_call_target="tpu_custom_call" | custom-call | tf_op jit(solution)/shard_map/pallas_call | solution.py:518
  369.4 17.0 %reduce-scatter.4.cloned.1.call-done = bf16[14080,128]{1,0:T(8,128)(2,1)} async-done(((bf16[28160,128]{1,0:T(8,128)(2,1)}), bf16[14080,128]{1,0:T(8,128)(2,1)}) %reduce-scatter.4.cloned.1.call-update) | async-done | bytes 3604496 | tf_op jit(solution)/shard_map/reduce_scatter | solution.py:726
  386.6 52.2 %reduce-scatter.6.cloned.1.call-done = bf16[3520,128]{1,0:T(8,128)(2,1)} async-done(((bf16[14080,128]{1,0:T(8,128)(2,1)}), bf16[3520,128]{1,0:T(8,128)(2,1)}) %reduce-scatter.6.cloned.1.call-update) | async-done | bytes 901136 | tf_op jit(solution)/shard_map/reduce_scatter | solution.py:726
  451.3 7.1 %collective-permute-done.15.up = bf16[5,64,640]{2,1,0:T(8,128)(2,1)S(1)} collective-permute-done((bf16[5,64,640]{2,1,0:T(8,128)(2,1)S(1)}, bf16[5,64,640]{2,1,0:T(8,128)(2,1)S(1)}, u32[]{:S(2)}, u32[]{:S(2)}) %collective-permute-start.15) | collective-permute-done | bytes 409632 | tf_op jit(solution)/shard_map/ppermute | solution.py:553
  458.4 11.6 %collective-permute-done.16.down = bf16[5,64,640]{2,1,0:T(8,128)(2,1)S(1)} collective-permute-done((bf16[5,64,640]{2,1,0:T(8,128)(2,1)S(1)}, bf16[5,64,640]{2,1,0:T(8,128)(2,1)S(1)}, u32[]{:S(2)}, u32[]{:S(2)}) %collective-permute-start.16) | collective-permute-done | bytes 409632 | tf_op jit(solution)/shard_map/ppermute | solution.py:554
  470.8 8.0 %shard_map.191 = f32[960,256]{1,0:T(8,128)} custom-call(s32[1]{0:T(128)} %bitcast.2.place_ref, f32[15]{0:T(128)} %reshape.121.valid_ref, bf16[3,5,64,640]{3,2,1,0:T(8,128)(2,1)} %get-tuple-element.99.ds_ref, bf16[5,64,640]{2,1,0:T(8,128)(2,1)} %copy-done.12, bf16[5,64,640]{2,1,0:T(8,128)(2,1)} %copy-done.13, bf16[3,64,640]{2,1,0:T(8,128)(2,1)} %copy-done.15, ...), custom_call_target="tpu_custom_call" | custom-call | tf_op jit(solution)/shard_map/pallas_call | solution.py:518
  (199 shorter events, 82.9 us)
Async XLA Ops:
  7.2 83.2 %all-gather.2.cloned.1.call-start = ((), (), s32[]{:S(2)}) async-start(), calls=%async_computation.11 | async-start | bytes 7434240 | tf_op jit(solution)/shard_map/all_gather | solution.py:582
  11.0 93.2 %copy-start = (bf16[3,5,64,256]{3,2,1,0:T(8,128)(2,1)}, bf16[3,5,64,256]{3,2,1,0:T(8,128)(2,1)S(1)}, u32[]{:S(2)}) copy-start(bf16[3,5,64,256]{3,2,1,0:T(8,128)(2,1)S(1)} %bitcast_multiply_fusion.1.tile_ref) | copy-start | bytes 1474564
  11.1 93.1 %collective-permute-start.4 = (bf16[64,256]{1,0:T(8,128)(2,1)S(1)}, bf16[64,256]{1,0:T(8,128)(2,1)S(1)}, u32[]{:S(2)}, u32[]{:S(2)}) collective-permute-start(bf16[64,256]{1,0:T(8,128)(2,1)S(1)} %get-tuple-element.124), channel_id=1, source_target_pairs={{2,1},{3,0},{4,3},{5,2},{6,5},{7,4},{10,9},{11,8},{12,11},{13,10},... | collective-permute-start | bytes 98312 | tf_op jit(solution)/shard_map/ppermute | solution.py:556
  12.5 91.7 %collective-permute-start.3 = (bf16[64,256]{1,0:T(8,128)(2,1)S(1)}, bf16[64,256]{1,0:T(8,128)(2,1)S(1)}, u32[]{:S(2)}, u32[]{:S(2)}) collective-permute-start(bf16[64,256]{1,0:T(8,128)(2,1)S(1)} %get-tuple-element.125), channel_id=1, source_target_pairs={{0,3},{1,2},{2,5},{3,4},{4,7},{5,6},{8,11},{9,10},{10,13},{11,12},... | collective-permute-start | bytes 98312 | tf_op jit(solution)/shard_map/ppermute | solution.py:555
  17.5 86.8 %collective-permute-start.2 = (bf16[3,64,256]{2,1,0:T(8,128)(2,1)S(1)}, bf16[3,64,256]{2,1,0:T(8,128)(2,1)S(1)}, u32[]{:S(2)}, u32[]{:S(2)}) collective-permute-start(bf16[3,64,256]{2,1,0:T(8,128)(2,1)S(1)} %dynamic-slice_bitcast_fusion), channel_id=1, source_target_pairs={{0,1},{1,0},{2,3},{3,2},{4,5},{5,4},{6,7},{7,6},{8,9},{9,8},{10,11... | collective-permute-start | bytes 294920 | tf_op jit(solution)/shard_map/ppermute | solution.py:557
  18.2 86.0 %collective-permute-start.1 = (bf16[5,64,256]{2,1,0:T(8,128)(2,1)S(1)}, bf16[5,64,256]{2,1,0:T(8,128)(2,1)S(1)}, u32[]{:S(2)}, u32[]{:S(2)}) collective-permute-start(bf16[5,64,256]{2,1,0:T(8,128)(2,1)S(1)} %get-tuple-element.126), channel_id=1, source_target_pairs={{2,0},{4,2},{6,4},{3,1},{5,3},{7,5},{10,8},{12,10},{14,12},{11,9},... | collective-permute-start | bytes 491528 | tf_op jit(solution)/shard_map/ppermute | solution.py:554
  19.5 84.7 %collective-permute-start = (bf16[5,64,256]{2,1,0:T(8,128)(2,1)S(1)}, bf16[5,64,256]{2,1,0:T(8,128)(2,1)S(1)}, u32[]{:S(2)}, u32[]{:S(2)}) collective-permute-start(bf16[5,64,256]{2,1,0:T(8,128)(2,1)S(1)} %get-tuple-element.127), channel_id=1, source_target_pairs={{0,2},{2,4},{4,6},{1,3},{3,5},{5,7},{8,10},{10,12},{12,14},{9,11},... | collective-permute-start | bytes 491528 | tf_op jit(solution)/shard_map/ppermute | solution.py:553
  113.7 11.9 %all-to-all-start = ((f32[32,1,1408]{2,1,0:T(1,128)}), f32[32,1,1408]{2,1,0:T(1,128)S(1)}, u32[]{:S(2)}, u32[]{:S(2)}) async-start(f32[32,1,1408]{2,1,0:T(1,128)} %get-tuple-element.64), calls=%async_computation | async-start | bytes 360448 | tf_op jit(solution)/shard_map/all_to_all | solution.py:539
  147.7 23.7 %collective-permute-start.5 = (bf16[5,64,256]{2,1,0:T(8,128)(2,1)}, bf16[5,64,256]{2,1,0:T(8,128)(2,1)S(1)}, u32[]{:S(2)}, u32[]{:S(2)}) collective-permute-start(bf16[5,64,256]{2,1,0:T(8,128)(2,1)} %get-tuple-element.69), channel_id=1, source_target_pairs={{0,2},{2,4},{4,6},{1,3},{3,5},{5,7},{8,10},{10,12},{12,14},{9,11},... | collective-permute-start | bytes 491528 | tf_op jit(solution)/shard_map/ppermute | solution.py:553
  150.0 21.4 %collective-permute-start.6 = (bf16[5,64,256]{2,1,0:T(8,128)(2,1)}, bf16[5,64,256]{2,1,0:T(8,128)(2,1)S(1)}, u32[]{:S(2)}, u32[]{:S(2)}) collective-permute-start(bf16[5,64,256]{2,1,0:T(8,128)(2,1)} %get-tuple-element.70), channel_id=1, source_target_pairs={{2,0},{4,2},{6,4},{3,1},{5,3},{7,5},{10,8},{12,10},{14,12},{11,9},... | collective-permute-start | bytes 491528 | tf_op jit(solution)/shard_map/ppermute | solution.py:554
  151.3 20.0 %collective-permute-start.7 = (bf16[3,64,256]{2,1,0:T(8,128)(2,1)}, bf16[3,64,256]{2,1,0:T(8,128)(2,1)S(1)}, u32[]{:S(2)}, u32[]{:S(2)}) collective-permute-start(bf16[3,64,256]{2,1,0:T(8,128)(2,1)} %get-tuple-element.71), channel_id=1, source_target_pairs={{0,1},{1,0},{2,3},{3,2},{4,5},{5,4},{6,7},{7,6},{8,9},{9,8},{10,11... | collective-permute-start | bytes 294920 | tf_op jit(solution)/shard_map/ppermute | solution.py:557
  151.4 19.9 %collective-permute-start.8 = (bf16[64,256]{1,0:T(8,128)(2,1)}, bf16[64,256]{1,0:T(8,128)(2,1)S(1)}, u32[]{:S(2)}, u32[]{:S(2)}) collective-permute-start(bf16[64,256]{1,0:T(8,128)(2,1)} %get-tuple-element.72), channel_id=1, source_target_pairs={{0,3},{1,2},{2,5},{3,4},{4,7},{5,6},{8,11},{9,10},{10,13},{11,12},... | collective-permute-start | bytes 98312 | tf_op jit(solution)/shard_map/ppermute | solution.py:555
  156.1 15.3 %collective-permute-start.9 = (bf16[64,256]{1,0:T(8,128)(2,1)}, bf16[64,256]{1,0:T(8,128)(2,1)S(1)}, u32[]{:S(2)}, u32[]{:S(2)}) collective-permute-start(bf16[64,256]{1,0:T(8,128)(2,1)} %get-tuple-element.73), channel_id=1, source_target_pairs={{2,1},{3,0},{4,3},{5,2},{6,5},{7,4},{10,9},{11,8},{12,11},{13,10},... | collective-permute-start | bytes 98312 | tf_op jit(solution)/shard_map/ppermute | solution.py:556
  180.9 13.8 %all-to-all-start.2 = ((f32[32,1,1408]{2,1,0:T(1,128)}), f32[32,1,1408]{2,1,0:T(1,128)S(1)}, u32[]{:S(2)}, u32[]{:S(2)}) async-start(f32[32,1,1408]{2,1,0:T(1,128)} %get-tuple-element.76), calls=%async_computation.2 | async-start | bytes 360448 | tf_op jit(solution)/shard_map/all_to_all | solution.py:539
  203.2 10.2 %all-to-all-start.3 = ((f32[32,1,640]{2,1,0:T(1,128)}), f32[32,1,640]{2,1,0:T(1,128)S(1)}, u32[]{:S(2)}, u32[]{:S(2)}) async-start(f32[32,1,640]{2,1,0:T(1,128)} %get-tuple-element.79), calls=%async_computation.3 | async-start | bytes 163840 | tf_op jit(solution)/shard_map/all_to_all | solution.py:539
  253.3 24.3 %collective-permute-start.10 = (bf16[5,64,640]{2,1,0:T(8,128)(2,1)}, bf16[5,64,640]{2,1,0:T(8,128)(2,1)S(1)}, u32[]{:S(2)}, u32[]{:S(2)}) collective-permute-start(bf16[5,64,640]{2,1,0:T(8,128)(2,1)} %get-tuple-element.88), channel_id=1, source_target_pairs={{0,2},{2,4},{4,6},{1,3},{3,5},{5,7},{8,10},{10,12},{12,14},{9,11},... | collective-permute-start | bytes 1228808 | tf_op jit(solution)/shard_map/ppermute | solution.py:553
  255.8 21.8 %collective-permute-start.11 = (bf16[5,64,640]{2,1,0:T(8,128)(2,1)}, bf16[5,64,640]{2,1,0:T(8,128)(2,1)S(1)}, u32[]{:S(2)}, u32[]{:S(2)}) collective-permute-start(bf16[5,64,640]{2,1,0:T(8,128)(2,1)} %get-tuple-element.89), channel_id=1, source_target_pairs={{2,0},{4,2},{6,4},{3,1},{5,3},{7,5},{10,8},{12,10},{14,12},{11,9},... | collective-permute-start | bytes 1228808 | tf_op jit(solution)/shard_map/ppermute | solution.py:554
  257.1 20.5 %collective-permute-start.12 = (bf16[3,64,640]{2,1,0:T(8,128)(2,1)}, bf16[3,64,640]{2,1,0:T(8,128)(2,1)S(1)}, u32[]{:S(2)}, u32[]{:S(2)}) collective-permute-start(bf16[3,64,640]{2,1,0:T(8,128)(2,1)} %get-tuple-element.90), channel_id=1, source_target_pairs={{0,1},{1,0},{2,3},{3,2},{4,5},{5,4},{6,7},{7,6},{8,9},{9,8},{10,11... | collective-permute-start | bytes 737288 | tf_op jit(solution)/shard_map/ppermute | solution.py:557
  257.2 9.7 %collective-permute-start.13 = (bf16[64,640]{1,0:T(8,128)(2,1)}, bf16[64,640]{1,0:T(8,128)(2,1)S(1)}, u32[]{:S(2)}, u32[]{:S(2)}) collective-permute-start(bf16[64,640]{1,0:T(8,128)(2,1)} %get-tuple-element.91), channel_id=1, source_target_pairs={{0,3},{1,2},{2,5},{3,4},{4,7},{5,6},{8,11},{9,10},{10,13},{11,12},... | collective-permute-start | bytes 245768 | tf_op jit(solution)/shard_map/ppermute | solution.py:555
  261.8 15.8 %collective-permute-start.14 = (bf16[64,640]{1,0:T(8,128)(2,1)}, bf16[64,640]{1,0:T(8,128)(2,1)S(1)}, u32[]{:S(2)}, u32[]{:S(2)}) collective-permute-start(bf16[64,640]{1,0:T(8,128)(2,1)} %get-tuple-element.92), channel_id=1, source_target_pairs={{2,1},{3,0},{4,3},{5,2},{6,5},{7,4},{10,9},{11,8},{12,11},{13,10},... | collective-permute-start | bytes 245768 | tf_op jit(solution)/shard_map/ppermute | solution.py:556
  306.3 20.1 %all-to-all-start.7 = ((f32[32,1,1280]{2,1,0:T(1,128)}), f32[32,1,1280]{2,1,0:T(1,128)S(1)}, u32[]{:S(2)}, u32[]{:S(2)}) async-start(f32[32,1,1280]{2,1,0:T(1,128)} %get-tuple-element.98), calls=%async_computation.7 | async-start | bytes 327680 | tf_op jit(solution)/shard_map/all_to_all | solution.py:539
  308.9 77.5 %reduce-scatter.4.cloned.1.call-start = ((), (), s32[]{:S(2)}) async-start(), calls=%async_computation.12 | async-start | bytes 10813440 | tf_op jit(solution)/shard_map/reduce_scatter | solution.py:726
  369.3 69.5 %copy-start.3 = (f32[960,256]{1,0:T(8,128)S(1)}, f32[960,256]{1,0:T(8,128)}, u32[]{:S(2)}) copy-start(f32[960,256]{1,0:T(8,128)} %get-tuple-element.80) | copy-start | bytes 2949124
  369.3 69.5 %reduce-scatter.6.cloned.1.call-start = ((), (), s32[]{:S(2)}) async-start(), calls=%async_computation.13 | async-start | bytes 4505600 | tf_op jit(solution)/shard_map/reduce_scatter | solution.py:726
  386.5 64.1 %copy-start.33 = (f32[2,1664]{1,0:T(2,128)S(1)}, f32[2,1664]{1,0:T(2,128)}, u32[]{:S(2)}) copy-start(f32[2,1664]{1,0:T(2,128)} %param.21) | copy-start | bytes 39940
  386.5 64.1 %copy-start.34 = (f32[2,1664]{1,0:T(2,128)S(1)}, f32[2,1664]{1,0:T(2,128)}, u32[]{:S(2)}) copy-start(f32[2,1664]{1,0:T(2,128)} %param.20) | copy-start | bytes 39940
  386.5 94.9 %reduce-scatter.8.cloned.1.call-start = ((), (), s32[]{:S(2)}) async-start(), calls=%async_computation.14 | async-start | bytes 1126400 | tf_op jit(solution)/shard_map/reduce_scatter | solution.py:726
  440.1 11.1 %collective-permute-start.18 = (bf16[64,640]{1,0:T(8,128)(2,1)S(1)}, bf16[64,640]{1,0:T(8,128)(2,1)S(1)}, u32[]{:S(2)}, u32[]{:S(2)}) collective-permute-start(bf16[64,640]{1,0:T(8,128)(2,1)S(1)} %copy-done.45), channel_id=1, source_target_pairs={{0,3},{1,2},{2,5},{3,4},{4,7},{5,6},{8,11},{9,10},{10,13},{11,12},... | collective-permute-start | bytes 245768 | tf_op jit(solution)/shard_map/ppermute | solution.py:555
  442.8 8.4 %collective-permute-start.19 = (bf16[64,640]{1,0:T(8,128)(2,1)S(1)}, bf16[64,640]{1,0:T(8,128)(2,1)S(1)}, u32[]{:S(2)}, u32[]{:S(2)}) collective-permute-start(bf16[64,640]{1,0:T(8,128)(2,1)S(1)} %copy-done.44), channel_id=1, source_target_pairs={{2,1},{3,0},{4,3},{5,2},{6,5},{7,4},{10,9},{11,8},{12,11},{13,10},... | collective-permute-start | bytes 245768 | tf_op jit(solution)/shard_map/ppermute | solution.py:556
  444.2 7.1 %collective-permute-start.17 = (bf16[3,64,640]{2,1,0:T(8,128)(2,1)S(1)}, bf16[3,64,640]{2,1,0:T(8,128)(2,1)S(1)}, u32[]{:S(2)}, u32[]{:S(2)}) collective-permute-start(bf16[3,64,640]{2,1,0:T(8,128)(2,1)S(1)} %copy-done.43), channel_id=1, source_target_pairs={{0,1},{1,0},{2,3},{3,2},{4,5},{5,4},{6,7},{7,6},{8,9},{9,8},{10,11... | collective-permute-start | bytes 737288 | tf_op jit(solution)/shard_map/ppermute | solution.py:557
  444.9 13.5 %collective-permute-start.15 = (bf16[5,64,640]{2,1,0:T(8,128)(2,1)S(1)}, bf16[5,64,640]{2,1,0:T(8,128)(2,1)S(1)}, u32[]{:S(2)}, u32[]{:S(2)}) collective-permute-start(bf16[5,64,640]{2,1,0:T(8,128)(2,1)S(1)} %copy-done.42), channel_id=1, source_target_pairs={{0,2},{2,4},{4,6},{1,3},{3,5},{5,7},{8,10},{10,12},{12,14},{9,11},... | collective-permute-start | bytes 1228808 | tf_op jit(solution)/shard_map/ppermute | solution.py:553
  449.1 20.9 %collective-permute-start.16 = (bf16[5,64,640]{2,1,0:T(8,128)(2,1)S(1)}, bf16[5,64,640]{2,1,0:T(8,128)(2,1)S(1)}, u32[]{:S(2)}, u32[]{:S(2)}) collective-permute-start(bf16[5,64,640]{2,1,0:T(8,128)(2,1)S(1)} %copy-done.41), channel_id=1, source_target_pairs={{2,0},{4,2},{6,4},{3,1},{5,3},{7,5},{10,8},{12,10},{14,12},{11,9},... | collective-permute-start | bytes 1228808 | tf_op jit(solution)/shard_map/ppermute | solution.py:554
  (42 other events, 755.9 us)
Sparse Core Ops, SparseCore 0:
  11.5 78.8 all-gather.1
  369.4 16.9 reduce-scatter.3
  389.8 48.9 reduce-scatter.5
  441.1 25.0 reduce-scatter.7
